TPU v7x, 512 devices: a whole 4x4x16 slice. The times are simulated.
512 devices in a mesh: lon: 16 (over z_hi, y, core), lat: 32 (over z_lo, x).
Axes of the slice: x: 4, y: 4, z: 16 (z_hi: 2, z_lo: 8; z = z_hi * 8 + z_lo), core: 2. Of those that a mesh axis runs over, the one named last changes fastest.
Arguments:
- coarse: bfloat16 [2048, 65536], P('lat', 'lon'), may hold values from -6 to 6
- ocean_mask: int32 [2048], replicated, may hold values from 0 to 1, as said below
- band_plan: int32 [2048], replicated, may hold values from 0 to 31, as said below
- up_weight: bfloat16 [3, 3, 64, 64], replicated, may hold values from -0.75 to 0.75
- up_bias: float32 [64], replicated, may hold values from -3 to 3
- first_weight: bfloat16 [3, 3, 64, 64], replicated, may hold values from -0.25 to 0.25
- first_bias: float32 [64], replicated, may hold values from -3 to 3
- second_weight: bfloat16 [3, 3, 64, 64], replicated, may hold values from -0.25 to 0.25
- second_bias: float32 [64], replicated, may hold values from -3 to 3
- head_weight: bfloat16 [64, 4], replicated, may hold values from -0.75 to 0.75
- head_bias: float32 [4], replicated, may hold values from -3 to 3
Outputs:
- fields: float32 [1024, 3, 12288], P('lat', None, 'lon')
Inputs may be any that keep to these rules, and one draw needn't show every extreme that they name: `ocean_mask`: exactly 1024 rows are ocean; the first and the last of the 64 rows of every lat index are ocean; every lat index holds 2 to 62 ocean rows, and some lat index holds exactly 62 of them in every draw. `band_plan`: ocean rows, taken in increasing order, go to the bands in a cyclic order of all 32 bands, so each band receives exactly 32 ocean rows and the rows of one lat index send at most 2 ocean rows to one band, a most that is reached in every draw; a land row holds the band of its own lat index.
All inputs are finite; a program needn't handle non-finite values.
Results may differ from a plain program's by a relative error of at most 0.0075.
Values may be sent and summed in bfloat16 or wider, within the bound.
A program may use at most 64 MiB of HBM per device.

v0:
```python
from functools import partial

import jax
import jax.numpy as jnp
from jax import lax
from jax.sharding import PartitionSpec as P


def padded(block, sides, width):
    for axis, dim in sides:
        count = lax.axis_size(axis)
        forward = [(i, i + 1) for i in range(count - 1)]
        backward = [(target, source) for source, target in forward]
        low = lax.ppermute(
            lax.slice_in_dim(block, block.shape[dim] - width, None, axis=dim), axis, forward
        )
        high = lax.ppermute(lax.slice_in_dim(block, 0, width, axis=dim), axis, backward)
        block = jnp.concatenate([low, block, high], axis=dim)
    return block


def shifted(block, axis, distance):
    devices = range(lax.axis_size(axis))
    route = [((i - distance) % len(devices), i) for i in devices]
    return lax.ppermute(block, axis, route)


def gelu_tanh(values):
    return jax.nn.gelu(values, approximate=True)


def conv_plain(image, weight):
    return lax.conv_general_dilated(
        image[None],
        weight,
        (1, 1),
        "VALID",
        dimension_numbers=("NHWC", "HWIO", "NHWC"),
        preferred_element_type=jnp.float32,
    )[0]


def expand_block(
    patch_in,
    row_masks,
    up_weight,
    up_bias,
    first_weight,
    first_bias,
    second_weight,
    second_bias,
    head_weight,
    head_bias,
):
    channels = up_weight.shape[2]
    fields_count = head_weight.shape[1]
    block_rows = patch_in.shape[0] - 2
    block_cols = patch_in.shape[1] // channels - 2
    coarse_grid = patch_in.reshape(block_rows + 2, block_cols + 2, channels)
    lifted = lax.conv_general_dilated(
        coarse_grid[None],
        up_weight[::-1, ::-1],
        (1, 1),
        ((2, 2), (2, 2)),
        lhs_dilation=(3, 3),
        dimension_numbers=("NHWC", "HWIO", "NHWC"),
        preferred_element_type=jnp.float32,
    )[0]
    lifted = lifted + up_bias
    fine_mask = jnp.repeat(row_masks, 3)[:, None, None]
    layer_zero = (gelu_tanh(lifted) * fine_mask).astype(jnp.bfloat16)
    layer_zero = layer_zero[1:-1, 1:-1]
    second = gelu_tanh(conv_plain(layer_zero, first_weight) + first_bias) * fine_mask[2:-2]
    second = second.astype(jnp.bfloat16)
    skip_path = second[1:-1, 1:-1].astype(jnp.float32)
    layer_two = (
        skip_path + gelu_tanh(conv_plain(second, second_weight) + second_bias)
    ) * fine_mask[3:-3]
    layer_two = layer_two.astype(jnp.bfloat16)
    result = (
        jnp.einsum("ikc,cf->ikf", layer_two, head_weight, preferred_element_type=jnp.float32)
        + head_bias
    )
    return result.reshape(block_rows, 3, 3 * block_cols * fields_count)


def body(
    coarse,
    ocean_mask,
    band_plan,
    up_weight,
    up_bias,
    first_weight,
    first_bias,
    second_weight,
    second_bias,
    head_weight,
    head_bias,
):
    channels = up_weight.shape[2]
    lat_count = lax.axis_size("lat")
    local_rows = coarse.shape[0]
    band_index = lax.axis_index("lat")
    send_rows = local_rows // lat_count
    capacity = local_rows // 2
    all_rows = local_rows * lat_count
    expand_one = partial(
        expand_block,
        up_weight=up_weight,
        up_bias=up_bias,
        first_weight=first_weight,
        first_bias=first_bias,
        second_weight=second_weight,
        second_bias=second_bias,
        head_weight=head_weight,
        head_bias=head_bias,
    )
    extended = padded(coarse, (("lat", 0),), 1)
    west_edge = shifted(extended[:, -channels:].reshape(-1), "lon", 1)
    east_edge = shifted(extended[:, :channels].reshape(-1), "lon", -1)
    patch_all = jnp.concatenate(
        [west_edge.reshape(-1, channels), extended, east_edge.reshape(-1, channels)], axis=1
    )
    ocean_float = jnp.concatenate(
        [jnp.zeros((1,), jnp.float32), ocean_mask.astype(jnp.float32), jnp.zeros((1,), jnp.float32)]
    )
    row_start = band_index * local_rows
    local_ocean = lax.dynamic_slice_in_dim(ocean_mask, row_start, local_rows)
    local_band = lax.dynamic_slice_in_dim(band_plan, row_start, local_rows)
    band_ids = jnp.arange(lat_count, dtype=jnp.int32)
    band_hits = (local_band[:, None] == band_ids[None, :]).astype(jnp.int32) * local_ocean[:, None]
    order_in = jnp.sum((jnp.cumsum(band_hits, axis=0) - 1) * band_hits, axis=1)
    slot_of = local_band * send_rows + order_in
    slot_ids = jnp.arange(local_rows, dtype=jnp.int32)
    pick_send = (slot_ids[:, None] == slot_of[None, :]) & (local_ocean[None, :] == 1)
    arrive = ocean_mask * (band_plan == band_index).astype(jnp.int32)
    arrive_rank = jnp.cumsum(arrive) - 1
    within = (jnp.cumsum(arrive.reshape(lat_count, local_rows), axis=1) - 1).reshape(all_rows)
    global_ids = jnp.arange(all_rows, dtype=jnp.int32)
    source_slot = global_ids // local_rows * send_rows + within
    target = (
        jnp.sum(
            arrive[None, :]
            * (source_slot[None, :] == slot_ids[:, None]).astype(jnp.int32)
            * (arrive_rank[None, :] + 1),
            axis=1,
        )
        - 1
    )
    keep_ids = jnp.arange(capacity, dtype=jnp.int32)
    pick_keep = target[None, :] == keep_ids[:, None]
    local_masks = lax.dynamic_slice_in_dim(ocean_float, row_start, local_rows + 2)

    def one_group(group_id):
        patch_rows = lax.dynamic_slice_in_dim(patch_all, group_id * 8, 10, 0)
        flag_rows = lax.dynamic_slice_in_dim(local_masks, group_id * 8, 10, 0)
        return expand_one(patch_rows, flag_rows)

    computed = lax.map(one_group, jnp.arange(local_rows // 8, dtype=jnp.int32))
    computed = computed.reshape(local_rows, -1)
    send_source = jnp.sum(pick_send.astype(jnp.int32) * (slot_ids[None, :] + 1), axis=1) - 1
    taken = jnp.take(computed, jnp.maximum(send_source, 0), axis=0)
    outgoing = jnp.where(send_source[:, None] >= 0, taken, jnp.zeros_like(taken))
    incoming = lax.all_to_all(
        outgoing.reshape(lat_count, send_rows, -1), "lat", split_axis=0, concat_axis=0, tiled=True
    )
    keep_source = jnp.sum(pick_keep.astype(jnp.int32) * (slot_ids[None, :] + 1), axis=1) - 1
    compacted = jnp.take(incoming.reshape(local_rows, -1), jnp.maximum(keep_source, 0), axis=0)
    return compacted.reshape(capacity, 3, -1)


def solution(mesh):
    in_specs = (P("lat", "lon"), P(), P(), P(), P(), P(), P(), P(), P(), P(), P())
    out_specs = P("lat", None, "lon")
    return jax.shard_map(body, mesh=mesh, in_specs=in_specs, out_specs=out_specs, check_vma=False)
```

profile of v0, /device:TPU:25, one launch (start us, length us, event | category | flops | bytes accessed | tf_op | source)
XLA Modules:
  0.0 408.8 jit_solution(6329801203491524743)
XLA Ops:
  2.3 4.0 collective-permute-start
  12.3 16.2 %collective-permute-start.2 = (bf16[4224]{0:T(1024)(128)(2,1)S(1)}, bf16[4224]{0:T(1024)(128)(2,1)S(1)}, u32[]{:S(2)}, u32[]{:S(2)}) collective-permute-start(bf16[4224]{0:T(1024)(128)(2,1)S(1)} %reshape.173), channel_id=1, source_target_pairs={{480,0},{0,32},{32,64},{64,96},{96,128},{128,160},{160,192},{192,2... | collective-permute-start | bytes 25352 | tf_op jit(solution)/shard_map/ppermute | solution.py:25
  32.7 11.6 %collective-permute-done.3 = bf16[4224]{0:T(1024)(128)(2,1)S(1)} collective-permute-done((bf16[4224]{0:T(1024)(128)(2,1)S(1)}, bf16[4224]{0:T(1024)(128)(2,1)S(1)}, u32[]{:S(2)}, u32[]{:S(2)}) %collective-permute-start.3) | collective-permute-done | bytes 8480 | tf_op jit(solution)/shard_map/ppermute | solution.py:25
  46.0 327.1 %while.10 = (s32[]{:T(128)}, f32[8,8,3,768]{3,2,1,0:T(4,128)}, s32[8]{0:T(128)S(1)}, bf16[66,4224]{1,0:T(8,128)(2,1)}, bf16[3,3,64,64]{3,2,1,0:T(8,128)(2,1)S(1)...) while((s32[]{:T(128)}, f32[8,8,3,768]{3,2,1,0:T(4,128)}, ...), condition=%wide.region_9.10_spmd, body=%wide.region_8.9_spmd.sunk | while | flops 813244416 | bytes 45383660 | solution.py:159
  50.6 2.6 fusion.100
  53.4 3.0 fusion.101
  64.8 3.3 copy.60
  68.1 5.1 %copy.61 = f32[26,8,25,64]{2,1,3,0:T(8,128)} copy(f32[26,8,25,64]{3,1,2,0:T(8,128)S(1)} %convolution_select_fusion.5) | data formatting | bytes 2662400 | tf_op jit(solution)/shard_map/while/body/eval_jaxpr/conv_general_dilated | solution.py:33
  73.2 4.5 %reshape.244 = f32[26,1,200,64]{2,3,0,1:T(8,128)S(1)} reshape(f32[26,8,25,64]{2,1,3,0:T(8,128)} %copy.61) | data formatting | bytes 2662400 | tf_op jit(solution)/shard_map/while/body/eval_jaxpr/conv_general_dilated | solution.py:33
  80.4 3.1 convolution_add_fusion.2
  94.2 3.0 fusion.101
  105.6 3.3 copy.60
  108.9 5.1 %copy.61 = f32[26,8,25,64]{2,1,3,0:T(8,128)} copy(f32[26,8,25,64]{3,1,2,0:T(8,128)S(1)} %convolution_select_fusion.5) | data formatting | bytes 2662400 | tf_op jit(solution)/shard_map/while/body/eval_jaxpr/conv_general_dilated | solution.py:33
  114.0 4.5 %reshape.244 = f32[26,1,200,64]{2,3,0,1:T(8,128)S(1)} reshape(f32[26,8,25,64]{2,1,3,0:T(8,128)} %copy.61) | data formatting | bytes 2662400 | tf_op jit(solution)/shard_map/while/body/eval_jaxpr/conv_general_dilated | solution.py:33
  121.2 3.1 convolution_add_fusion.2
  135.1 3.0 fusion.101
  146.5 3.3 copy.60
  149.8 5.1 %copy.61 = f32[26,8,25,64]{2,1,3,0:T(8,128)} copy(f32[26,8,25,64]{3,1,2,0:T(8,128)S(1)} %convolution_select_fusion.5) | data formatting | bytes 2662400 | tf_op jit(solution)/shard_map/while/body/eval_jaxpr/conv_general_dilated | solution.py:33
  154.9 4.5 %reshape.244 = f32[26,1,200,64]{2,3,0,1:T(8,128)S(1)} reshape(f32[26,8,25,64]{2,1,3,0:T(8,128)} %copy.61) | data formatting | bytes 2662400 | tf_op jit(solution)/shard_map/while/body/eval_jaxpr/conv_general_dilated | solution.py:33
  162.1 3.1 convolution_add_fusion.2
  176.0 3.0 fusion.101
  187.4 3.3 copy.60
  190.7 5.1 %copy.61 = f32[26,8,25,64]{2,1,3,0:T(8,128)} copy(f32[26,8,25,64]{3,1,2,0:T(8,128)S(1)} %convolution_select_fusion.5) | data formatting | bytes 2662400 | tf_op jit(solution)/shard_map/while/body/eval_jaxpr/conv_general_dilated | solution.py:33
  195.7 4.5 %reshape.244 = f32[26,1,200,64]{2,3,0,1:T(8,128)S(1)} reshape(f32[26,8,25,64]{2,1,3,0:T(8,128)} %copy.61) | data formatting | bytes 2662400 | tf_op jit(solution)/shard_map/while/body/eval_jaxpr/conv_general_dilated | solution.py:33
  203.0 3.1 convolution_add_fusion.2
  216.8 3.0 fusion.101
  228.2 3.3 copy.60
  231.5 5.1 %copy.61 = f32[26,8,25,64]{2,1,3,0:T(8,128)} copy(f32[26,8,25,64]{3,1,2,0:T(8,128)S(1)} %convolution_select_fusion.5) | data formatting | bytes 2662400 | tf_op jit(solution)/shard_map/while/body/eval_jaxpr/conv_general_dilated | solution.py:33
  236.6 4.5 %reshape.244 = f32[26,1,200,64]{2,3,0,1:T(8,128)S(1)} reshape(f32[26,8,25,64]{2,1,3,0:T(8,128)} %copy.61) | data formatting | bytes 2662400 | tf_op jit(solution)/shard_map/while/body/eval_jaxpr/conv_general_dilated | solution.py:33
  243.8 3.1 convolution_add_fusion.2
  257.7 3.0 fusion.101
  269.1 3.3 copy.60
  272.4 5.1 %copy.61 = f32[26,8,25,64]{2,1,3,0:T(8,128)} copy(f32[26,8,25,64]{3,1,2,0:T(8,128)S(1)} %convolution_select_fusion.5) | data formatting | bytes 2662400 | tf_op jit(solution)/shard_map/while/body/eval_jaxpr/conv_general_dilated | solution.py:33
  277.5 4.5 %reshape.244 = f32[26,1,200,64]{2,3,0,1:T(8,128)S(1)} reshape(f32[26,8,25,64]{2,1,3,0:T(8,128)} %copy.61) | data formatting | bytes 2662400 | tf_op jit(solution)/shard_map/while/body/eval_jaxpr/conv_general_dilated | solution.py:33
  284.7 3.1 convolution_add_fusion.2
  298.6 3.0 fusion.101
  310.0 3.3 copy.60
  313.3 5.1 %copy.61 = f32[26,8,25,64]{2,1,3,0:T(8,128)} copy(f32[26,8,25,64]{3,1,2,0:T(8,128)S(1)} %convolution_select_fusion.5) | data formatting | bytes 2662400 | tf_op jit(solution)/shard_map/while/body/eval_jaxpr/conv_general_dilated | solution.py:33
  318.4 4.5 %reshape.244 = f32[26,1,200,64]{2,3,0,1:T(8,128)S(1)} reshape(f32[26,8,25,64]{2,1,3,0:T(8,128)} %copy.61) | data formatting | bytes 2662400 | tf_op jit(solution)/shard_map/while/body/eval_jaxpr/conv_general_dilated | solution.py:33
  325.6 3.1 convolution_add_fusion.2
  336.6 2.6 fusion.100
  339.4 3.0 fusion.101
  350.8 3.3 copy.60
  354.1 5.1 %copy.61 = f32[26,8,25,64]{2,1,3,0:T(8,128)} copy(f32[26,8,25,64]{3,1,2,0:T(8,128)S(1)} %convolution_select_fusion.5) | data formatting | bytes 2662400 | tf_op jit(solution)/shard_map/while/body/eval_jaxpr/conv_general_dilated | solution.py:33
  359.2 4.5 %reshape.244 = f32[26,1,200,64]{2,3,0,1:T(8,128)S(1)} reshape(f32[26,8,25,64]{2,1,3,0:T(8,128)} %copy.61) | data formatting | bytes 2662400 | tf_op jit(solution)/shard_map/while/body/eval_jaxpr/conv_general_dilated | solution.py:33
  366.4 3.1 convolution_add_fusion.2
  377.0 9.0 %all-to-all-start = ((f32[32,2,2304]{2,1,0:T(2,128)}), f32[32,2,2304]{2,1,0:T(2,128)S(1)}, u32[]{:S(2)}, u32[]{:S(2)}) async-start(f32[32,2,2304]{2,1,0:T(2,128)} %select_select_fusion), calls=%async_computation | async-start | bytes 1179648 | tf_op jit(solution)/shard_map/all_to_all | solution.py:164
  387.3 19.3 %all-to-all-done = f32[32,2,2304]{2,1,0:T(2,128)S(1)} async-done(((f32[32,2,2304]{2,1,0:T(2,128)}), f32[32,2,2304]{2,1,0:T(2,128)S(1)}, u32[]{:S(2)}, u32[]{:S(2)}) %all-to-all-start) | async-done | bytes 589856 | tf_op jit(solution)/shard_map/all_to_all | solution.py:164
  (545 shorter events, 184.5 us)
Async XLA Ops:
  0.0 46.0 %copy-start.2 = (pred[8,27]{0,1:T(8,128)(4,1)S(1)}, pred[8,27]{0,1:T(8,128)(4,1)}, u32[]{:S(2)}) copy-start(pred[8,27]{0,1:T(8,128)(4,1)} %constant.266) | copy-start | bytes 652
  0.0 46.0 %copy-start.4 = (pred[8,25]{0,1:T(8,128)(4,1)S(1)}, pred[8,25]{0,1:T(8,128)(4,1)}, u32[]{:S(2)}) copy-start(pred[8,25]{0,1:T(8,128)(4,1)} %constant.268) | copy-start | bytes 604
  0.0 46.0 %copy-start = (bf16[3,3,64,64]{3,2,1,0:T(8,128)(2,1)S(1)}, bf16[3,3,64,64]{3,2,1,0:T(8,128)(2,1)}, u32[]{:S(2)}) copy-start(bf16[3,3,64,64]{3,2,1,0:T(8,128)(2,1)} %param.16) | copy-start | bytes 221188
  0.0 46.0 %copy-start.10 = (f32[64]{0:T(128)S(1)}, f32[64]{0:T(128)}, u32[]{:S(2)}) copy-start(f32[64]{0:T(128)} %param.17) | copy-start | bytes 772
  0.0 46.0 %copy-start.6 = (f32[64]{0:T(128)S(1)}, f32[64]{0:T(128)}, u32[]{:S(2)}) copy-start(f32[64]{0:T(128)} %param.19) | copy-start | bytes 772
  1.0 9.5 %collective-permute-start.1 = (bf16[1,4096]{1,0:T(2,128)(2,1)S(1)}, bf16[1,4096]{1,0:T(2,128)(2,1)S(1)}, u32[]{:S(2)}, u32[]{:S(2)}) collective-permute-start(bf16[1,4096]{1,0:T(2,128)(2,1)S(1)} %get-tuple-element.108), channel_id=1, source_target_pairs={{1,0},{2,1},{3,2},{4,3},{5,4},{6,5},{7,6},{8,7},{9,8},{10,9},{11,1... | collective-permute-start | bytes 24584 | tf_op jit(solution)/shard_map/ppermute | solution.py:17
  2.3 8.2 %collective-permute-start = (bf16[1,4096]{1,0:T(2,128)(2,1)S(1)}, bf16[1,4096]{1,0:T(2,128)(2,1)S(1)}, u32[]{:S(2)}, u32[]{:S(2)}) collective-permute-start(bf16[1,4096]{1,0:T(2,128)(2,1)S(1)} %get-tuple-element.107), channel_id=1, source_target_pairs={{0,1},{1,2},{2,3},{3,4},{4,5},{5,6},{6,7},{7,8},{8,9},{9,10},{10,1... | collective-permute-start | bytes 24584 | tf_op jit(solution)/shard_map/ppermute | solution.py:14
  12.3 20.4 %collective-permute-start.2 = (bf16[4224]{0:T(1024)(128)(2,1)S(1)}, bf16[4224]{0:T(1024)(128)(2,1)S(1)}, u32[]{:S(2)}, u32[]{:S(2)}) collective-permute-start(bf16[4224]{0:T(1024)(128)(2,1)S(1)} %reshape.173), channel_id=1, source_target_pairs={{480,0},{0,32},{32,64},{64,96},{96,128},{128,160},{160,192},{192,2... | collective-permute-start | bytes 25352 | tf_op jit(solution)/shard_map/ppermute | solution.py:25
  28.6 15.8 %collective-permute-start.3 = (bf16[4224]{0:T(1024)(128)(2,1)S(1)}, bf16[4224]{0:T(1024)(128)(2,1)S(1)}, u32[]{:S(2)}, u32[]{:S(2)}) collective-permute-start(bf16[4224]{0:T(1024)(128)(2,1)S(1)} %reshape.175), channel_id=1, source_target_pairs={{32,0},{64,32},{96,64},{128,96},{160,128},{192,160},{224,192},{256... | collective-permute-start | bytes 25352 | tf_op jit(solution)/shard_map/ppermute | solution.py:25
  46.0 3.8 copy-start.20
  46.0 3.8 copy-start.22
  48.0 11.6 %copy-start.12 = (f32[26]{0:T(128)}, f32[26]{0:T(128)S(1)}, u32[]{:S(2)}) copy-start(f32[26]{0:T(128)S(1)} %slice_bitcast_fusion.4) | copy-start | bytes 316 | tf_op jit(solution)/shard_map/while
  84.2 2.6 copy-start.3
  86.9 3.8 copy-start.20
  86.9 3.8 copy-start.22
  88.9 11.6 %copy-start.12 = (f32[26]{0:T(128)}, f32[26]{0:T(128)S(1)}, u32[]{:S(2)}) copy-start(f32[26]{0:T(128)S(1)} %slice_bitcast_fusion.4) | copy-start | bytes 316 | tf_op jit(solution)/shard_map/while
  125.1 2.6 copy-start.3
  127.8 3.8 copy-start.20
  127.8 3.8 copy-start.22
  129.7 11.6 %copy-start.12 = (f32[26]{0:T(128)}, f32[26]{0:T(128)S(1)}, u32[]{:S(2)}) copy-start(f32[26]{0:T(128)S(1)} %slice_bitcast_fusion.4) | copy-start | bytes 316 | tf_op jit(solution)/shard_map/while
  165.9 2.6 copy-start.3
  168.6 3.8 copy-start.20
  168.6 3.8 copy-start.22
  170.6 11.6 %copy-start.12 = (f32[26]{0:T(128)}, f32[26]{0:T(128)S(1)}, u32[]{:S(2)}) copy-start(f32[26]{0:T(128)S(1)} %slice_bitcast_fusion.4) | copy-start | bytes 316 | tf_op jit(solution)/shard_map/while
  206.8 2.6 copy-start.3
  206.8 2.6 copy-start.5
  209.5 3.8 copy-start.20
  209.5 3.8 copy-start.22
  211.5 11.6 %copy-start.12 = (f32[26]{0:T(128)}, f32[26]{0:T(128)S(1)}, u32[]{:S(2)}) copy-start(f32[26]{0:T(128)S(1)} %slice_bitcast_fusion.4) | copy-start | bytes 316 | tf_op jit(solution)/shard_map/while
  247.7 2.6 copy-start.3
  250.4 3.8 copy-start.20
  250.4 3.8 copy-start.22
  252.3 11.6 %copy-start.12 = (f32[26]{0:T(128)}, f32[26]{0:T(128)S(1)}, u32[]{:S(2)}) copy-start(f32[26]{0:T(128)S(1)} %slice_bitcast_fusion.4) | copy-start | bytes 316 | tf_op jit(solution)/shard_map/while
  288.6 2.6 copy-start.3
  291.2 3.8 copy-start.20
  291.2 3.8 copy-start.22
  293.2 11.6 %copy-start.12 = (f32[26]{0:T(128)}, f32[26]{0:T(128)S(1)}, u32[]{:S(2)}) copy-start(f32[26]{0:T(128)S(1)} %slice_bitcast_fusion.4) | copy-start | bytes 316 | tf_op jit(solution)/shard_map/while
  329.4 2.6 copy-start.3
  329.4 2.6 copy-start.5
  329.4 2.6 copy-start.7
  332.1 3.8 copy-start.20
  332.1 3.8 copy-start.22
  334.1 11.5 %copy-start.12 = (f32[26]{0:T(128)}, f32[26]{0:T(128)S(1)}, u32[]{:S(2)}) copy-start(f32[26]{0:T(128)S(1)} %slice_bitcast_fusion.4) | copy-start | bytes 316 | tf_op jit(solution)/shard_map/while
  370.3 2.6 copy-start.3
  370.3 2.6 copy-start.5
  375.3 10.7 %copy-start.1 = (s32[2048]{0:T(1024)S(1)}, s32[2048]{0:T(1024)}, u32[]{:S(2)}) copy-start(s32[2048]{0:T(1024)} %get-tuple-element.109) | copy-start | bytes 24580
  375.3 11.8 %copy-start.17 = (s32[64]{0:T(128)S(1)}, s32[64]{0:T(128)}, u32[]{:S(2)}) copy-start(s32[64]{0:T(128)} %copy-done.16) | copy-start | bytes 772
  377.0 29.6 %all-to-all-start = ((f32[32,2,2304]{2,1,0:T(2,128)}), f32[32,2,2304]{2,1,0:T(2,128)S(1)}, u32[]{:S(2)}, u32[]{:S(2)}) async-start(f32[32,2,2304]{2,1,0:T(2,128)} %select_select_fusion), calls=%async_computation | async-start | bytes 1179648 | tf_op jit(solution)/shard_map/all_to_all | solution.py:164
  (79 other events, 157.3 us)
where the time goes:
time: 411 us; the launch traced here: 409 us
  local copies, waits for them, and re-layouts  197 us (48%)
  other arithmetic  80.6 us (20%)
  matrix products  60.4 us (15%)
  starting transfers between devices  32.4 us (8%)
  waiting for transfers between devices  30.9 us (8%)
  loops' own time  7.49 us (2%)
    conv_general_dilated x48, local copies, waits for them, and re-layouts, conv_plain(): lax.conv_general_dilated(image[None], weight, (1, 1), 'VALID', dimension_...  97.7 us
    mul x16, other arithmetic, gelu_tanh(): return jax.nn.gelu(values, approximate=True)  40.3 us
    while x232, local copies, waits for them, and re-layouts  32.7 us
    conv_general_dilated x16, matrix products, conv_plain(): lax.conv_general_dilated(image[None], weight, (1, 1), 'VALID', dimension_...  31.1 us
    dot_general x8, matrix products, expand_block(): jnp.einsum('ikc,cf->ikf', layer_two, head_weight, preferred_element_type=...  24.7 us
    broadcast_in_dim x8, other arithmetic, conv_plain(): image[None]  23.7 us
    all_to_all x1, waiting for transfers between devices, body(): lax.all_to_all(outgoing.reshape(lat_count, send_rows, -1), 'lat', split_a...  19.3 us
    ppermute x2, starting transfers between devices, shifted(): return lax.ppermute(block, axis, route)  18.1 us
  transfers between devices with their start and end apart: 5, of which 2 were waited for; matrix products, arithmetic and copies ran while one was open for 2% of the time, Pallas kernels for 0%

commit v1 on v0

v1 whole, which is shorter than its diff:
```python
from functools import partial

import jax
import jax.numpy as jnp
import numpy as np
from jax import lax
from jax.experimental import pallas as pl
from jax.experimental.pallas import tpu as pltpu
from jax.sharding import PartitionSpec as P

MESH = pl.DeviceIdType.MESH
BF = jnp.bfloat16
F32 = jnp.float32
ROWS = 64
SUB = 16
TILES = ROWS // SUB
LANES = 128
PAIRS = 32
GROUP = 11
CHUNKS = 3
SPAN = 32
SLOPE = float(np.sqrt(2.0 / np.pi))


def dot(a, b):
    return jnp.dot(a, b, preferred_element_type=F32)


def dot_t(a, b):
    return lax.dot_general(a, b, (((1,), (1,)), ((), ())), preferred_element_type=F32)


def iota(shape, dim):
    return lax.broadcasted_iota(jnp.int32, shape, dim)


def gelu_of_half(h):
    return h + h * jnp.tanh(h * (2 * SLOPE + (8 * 0.044715 * SLOPE) * (h * h)))


def place_of(m):
    return (m % SUB) * TILES + m // SUB


def store_layer(ref, at, a, value, masks):
    rounded = value.astype(BF)
    ref[at, a + 1] = rounded
    if a == 2:
        rolled = pltpu.roll(value[ROWS - SUB :], 1, 0).astype(BF)
        ref[at, 0, 0:SUB] = rolled * masks[0, 0:SUB]
        for t in range(1, TILES):
            low = t * SUB
            ref[at, 0, low : low + SUB] = rounded[low - SUB : low] * masks[0, low : low + SUB]
    if a == 0:
        for t in range(TILES - 1):
            low = t * SUB
            ref[at, 4, low : low + SUB] = (
                rounded[low + SUB : low + 2 * SUB] * masks[1, low : low + SUB]
            )
        rolled = pltpu.roll(value[:SUB], SUB - 1, 0).astype(BF)
        ref[at, 4, ROWS - SUB :] = rolled * masks[1, ROWS - SUB :]


def widen(weight_ref):
    channels = weight_ref.shape[-1]
    taps = weight_ref[...].reshape(-1, channels)
    row, lane = iota((channels, LANES), 0), iota((channels, LANES), 1)
    halves = []
    for shift in (0, channels):
        wide = dot(taps, (lane == row + shift).astype(BF)) * 0.5
        wide = wide.astype(BF)
        halves.append(
            [
                [wide[(p * 3 + q) * channels : (p * 3 + q + 1) * channels] for q in range(3)]
                for p in range(3)
            ]
        )
    return halves


def build_conv(weight_ref, w_pair, w_one, layer):
    low, high = widen(weight_ref)
    zero = jnp.zeros((256, LANES), BF)
    blocks = [
        jnp.concatenate(
            [low[p][0], low[p][1] + high[p][0], low[p][2] + high[p][1], high[p][2]], axis=0
        )
        for p in range(3)
    ]
    for i in range(4):
        at = slice(i * 256, (i + 1) * 256)
        w_pair[layer, at, 0:LANES] = blocks[i] if i < 3 else zero
        w_pair[layer, at, LANES:] = blocks[i - 1] if i > 0 else zero
    for i in range(3):
        w_one[layer, i * 256 : (i + 1) * 256, :] = blocks[i]


def build_up(weight_ref, w_up):
    low, high = widen(weight_ref)
    zero = jnp.zeros((64, LANES), BF)
    for a in range(3):
        first = [low[a][0] + high[a][1], low[a][2], zero]
        second = [zero, high[a][0], low[a][1] + high[a][2]]
        for n in range(3):
            at = slice(n * LANES, (n + 1) * LANES)
            w_up[a, 0:64, at] = first[n]
            w_up[a, 64:128, at] = second[n]


def build_head(weight_ref, w_head):
    fields = weight_ref.shape[1]
    row, lane = iota((fields, LANES), 0), iota((fields, LANES), 1)
    tiled = dot(weight_ref[...], (lane % fields == row).astype(BF))
    pixel = iota(tiled.shape, 1) // fields
    for p in range(16):
        for part, v in enumerate((0, 1, 1, 0)):
            block = jnp.where(pixel == 2 * p + v, tiled, 0.0).astype(BF)
            w_head[p, part * 64 : (part + 1) * 64, :] = block


def conv(ref, w_pair, w_one, bias, layer, at, count):
    pieces = [
        [ref[pl.ds(at + d, count), i].reshape(count * ROWS, LANES) for d in range(2)]
        for i in range(5)
    ]
    both = dot(jnp.concatenate(sum(pieces[:4], []), axis=1), w_pair[layer])
    last = dot(jnp.concatenate(sum(pieces[2:], []), axis=1), w_one[layer])
    rows = [both[:, :LANES], both[:, LANES:], last]
    return [gelu_of_half(z + bias) for z in rows]


def kernel(
    lat_count,
    lon_count,
    x_ref,
    ocean_ref,
    band_ref,
    up_weight,
    up_bias,
    first_weight,
    first_bias,
    second_weight,
    second_bias,
    head_weight,
    head_bias,
    out_ref,
    edge,
    halo,
    corner,
    side,
    xc,
    zero_layer,
    one_layer,
    grown,
    w_up,
    w_pair,
    w_one,
    w_head,
    masks,
    spread,
    gather,
    outgoing,
    incoming,
    halo_send,
    halo_recv,
    out_send,
    out_recv,
):
    me = lax.axis_index("lat")
    lon = lax.axis_index("lon")
    north, south = (me + lat_count - 1) % lat_count, (me + 1) % lat_count
    west, east = (lon + lon_count - 1) % lon_count, (lon + 1) % lon_count
    width = x_ref.shape[1]

    barrier = pltpu.get_barrier_semaphore()

    def greet(t, carry):
        pl.semaphore_signal(
            barrier,
            inc=1,
            device_id={"lat": (me + t) % lat_count, "lon": lon},
            device_id_type=MESH,
        )
        return carry

    lax.fori_loop(1, lat_count, greet, 0)
    others = [(me, west), (me, east)] + [(r, c) for r in (north, south) for c in (west, east)]
    for r, c in others:
        pl.semaphore_signal(
            barrier, inc=1, device_id={"lat": r, "lon": c}, device_id_type=MESH
        )

    edge[0] = x_ref[0:SUB, :].astype(F32)[0:1]
    edge[1] = x_ref[ROWS - SUB :, :].astype(F32)[SUB - 1 :]

    pl.semaphore_wait(barrier, lat_count - 1 + len(others))
    first, final = pl.ds(0, LANES), pl.ds(width - LANES, LANES)
    plan = [
        (edge.at[0], halo.at[1], north, lon),
        (edge.at[1], halo.at[0], south, lon),
        (x_ref.at[:, first], side.at[0], me, west),
        (x_ref.at[:, final], side.at[1], me, east),
        (edge.at[0, :, first], corner.at[1, 0], north, west),
        (edge.at[0, :, final], corner.at[1, 1], north, east),
        (edge.at[1, :, first], corner.at[0, 0], south, west),
        (edge.at[1, :, final], corner.at[0, 1], south, east),
    ]
    copies = []
    for n, (source, target, r, c) in enumerate(plan):
        copy = pltpu.make_async_remote_copy(
            src_ref=source,
            dst_ref=target,
            send_sem=halo_send.at[n],
            recv_sem=halo_recv.at[n],
            device_id={"lat": r, "lon": c},
            device_id_type=MESH,
        )
        copy.start()
        copies.append(copy)

    row, col = iota((ROWS, ROWS), 0), iota((ROWS, ROWS), 1)
    source = iota((LANES, ROWS), 0) == (me % 2) * ROWS + iota((LANES, ROWS), 1)
    source = source.astype(BF)
    ocean_all = ocean_ref[...].astype(F32).astype(BF)
    band_all = band_ref[...].astype(F32).astype(BF)
    half_rows = ocean_all.shape[0]
    mine = (iota((SUB, half_rows), 1) == me // 2).astype(BF)
    ocean_row = dot(dot(mine, ocean_all).astype(BF), source)[0:1]
    band_row = dot(dot(mine, band_all).astype(BF), source)[0:1]
    eye = (row == col).astype(F32)
    before = (row < col).astype(F32)
    ocean_col = jnp.sum(eye * ocean_row, axis=1, keepdims=True)
    band_col = jnp.sum(eye * band_row, axis=1, keepdims=True)
    order_row = jnp.sum(before * ocean_col, axis=0, keepdims=True) + 1.0
    order_col = jnp.sum((col < row).astype(F32) * ocean_row, axis=1, keepdims=True) + 1.0
    total = jnp.sum(ocean_row, axis=1, keepdims=True)
    place = place_of(row).astype(F32)
    pick = jnp.where(place == order_row, ocean_row, 0.0)
    top = (place[:, 0:1] == 0.0).astype(F32)
    bottom = (place[:, 0:1] == total + 1.0).astype(F32)
    has_north = jnp.where(me > 0, 1.0, 0.0)
    has_south = jnp.where(me < lat_count - 1, 1.0, 0.0)
    above = jnp.sum((row + 1 == col).astype(F32) * ocean_col, axis=0, keepdims=True)
    above = above + jnp.where(col[0:1] == 0, has_north, 0.0)
    below = jnp.sum((row == col + 1).astype(F32) * ocean_col, axis=0, keepdims=True)
    below = below + jnp.where(col[0:1] == ROWS - 1, has_south, 0.0)
    up_mask = jnp.sum(pick * above, axis=1, keepdims=True) + bottom
    down_mask = jnp.sum(pick * below, axis=1, keepdims=True) + top
    masks[0] = jnp.broadcast_to(up_mask, (ROWS, LANES)).astype(BF)
    masks[1] = jnp.broadcast_to(down_mask, (ROWS, LANES)).astype(BF)

    earlier = jnp.where(band_col == band_row, before, 0.0) * ocean_col
    turn_row = jnp.sum(earlier, axis=0, keepdims=True)
    line = iota((lat_count * SUB, ROWS), 0)
    slot = (line // SUB * 2 + line % SUB // 6).astype(F32)
    fits = (slot == band_row * 2.0 + turn_row) & (line % SUB < 12)
    leaves = jnp.where(fits, ocean_row, 0.0).astype(BF)
    lane = iota((ROWS, 6 * ROWS), 1)
    there = place_of(lane % ROWS).astype(F32) == order_col
    there = jnp.where(there, ocean_col, 0.0).astype(BF)
    moved = dot(leaves, there)
    line, lane = iota(moved.shape, 0), iota(moved.shape, 1)
    spread[...] = jnp.where(line % SUB % 6 == lane // ROWS, moved, 0.0).astype(BF)

    arrive = jnp.where(band_all.astype(F32) == me.astype(F32), ocean_all.astype(F32), 0.0)
    width_in = lat_count * SUB
    home = iota((LANES, width_in), 1) // SUB
    counts = dot(arrive.astype(BF), (iota((LANES, width_in), 0) // ROWS == home % 2).astype(BF))
    home = iota(counts.shape, 1) // SUB
    count_row = jnp.sum(
        jnp.where(iota(counts.shape, 0) == home // 2, counts, 0.0), axis=0, keepdims=True
    )
    sooner = jnp.where(iota(counts.shape, 0) < home // 2, counts, 0.0)
    other = dot(arrive.astype(BF), (iota((LANES, width_in), 0) // ROWS != iota((LANES, width_in), 1) // SUB % 2).astype(BF))
    sooner = sooner + jnp.where(iota(counts.shape, 0) < home // 2, other, 0.0)
    sooner = sooner + jnp.where(
        (iota(counts.shape, 0) == home // 2) & (home % 2 == 1), other, 0.0
    )
    base_row = jnp.sum(sooner, axis=0, keepdims=True)
    slots = out_ref.shape[0]
    shape = (2 * slots * 4, width_in)
    line, lane = iota(shape, 0), iota(shape, 1)
    turn = lane % SUB // 6
    part = lane % SUB % 6
    wanted = (line // (slots * 4)) * 3 + line % 4
    number = (line // 4 % slots - turn).astype(F32)
    hit = (number == base_row) & (turn.astype(F32) < count_row)
    hit = hit & (part == wanted) & (line % 4 < 3) & (lane % SUB < 12)
    gather[...] = jnp.where(hit, 1.0, 0.0).astype(BF)

    build_up(up_weight, w_up)
    build_conv(first_weight, w_pair, w_one, 0)
    build_conv(second_weight, w_pair, w_one, 1)
    build_head(head_weight, w_head)
    bias_up, bias_one, bias_two = (
        jnp.concatenate([b[...], b[...]], axis=1) * 0.5 for b in (up_bias, first_bias, second_bias)
    )
    bias_head = jnp.concatenate([head_bias[...]] * (LANES // head_bias.shape[1]), axis=1)

    for copy in copies:
        copy.wait()

    ends = iota((ROWS, SUB), 1)
    pick_ends = jnp.where(ends == 0, top, jnp.where(ends == 1, bottom, 0.0))
    pick_all = jnp.concatenate([pick.astype(BF), pick_ends.astype(BF)], axis=1)

    def two_rows(upper, lower):
        which = iota((SUB, upper.shape[1]), 0)
        return jnp.where(which == 0, upper, jnp.where(which == 1, lower, 0.0)).astype(BF)

    lifted = dot(
        pick_all, jnp.concatenate([x_ref[...], two_rows(halo[0], halo[1])], axis=0)
    ).astype(BF)
    for j in range(PAIRS):
        xc[j] = lifted[:, j * LANES : (j + 1) * LANES]
    low_lanes = iota((1, LANES), 1) < 64
    joined = jnp.where(low_lanes, side[0].astype(F32), side[1].astype(F32)).astype(BF)
    joined_ends = two_rows(
        jnp.where(low_lanes, corner[0, 0], corner[0, 1]),
        jnp.where(low_lanes, corner[1, 0], corner[1, 1]),
    )
    outer = dot(pick_all, jnp.concatenate([joined, joined_ends], axis=0)).astype(BF)
    for a in range(3):
        z = dot(outer, w_up[a])
        for n, at in ((2, 0), (0, 3 * PAIRS + 1)):
            grow = gelu_of_half(z[:, n * LANES : (n + 1) * LANES] + bias_up)
            store_layer(zero_layer, at, a, grow, masks)

    def chunk(c, carry):
        start = jnp.minimum(c * GROUP, PAIRS - GROUP)
        source = xc[pl.ds(start, GROUP)].reshape(GROUP * ROWS, LANES)
        for a in range(3):
            z = dot(source, w_up[a])
            for n in range(3):
                grow = gelu_of_half(z[:, n * LANES : (n + 1) * LANES] + bias_up)
                for j in range(GROUP):
                    value = grow[j * ROWS : (j + 1) * ROWS]
                    store_layer(zero_layer, 3 * (start + j) + 1 + n, a, value, masks)

        base = c * SPAN
        step = 11

        def first(g, carry):
            at = base + g * step
            rows = conv(zero_layer, w_pair, w_one, bias_one, 0, at, step)
            for a in range(3):
                for j in range(step):
                    store_layer(one_layer, at + j, a, rows[a][j * ROWS : (j + 1) * ROWS], masks)
            return carry

        lax.fori_loop(0, (SPAN + 1) // step, first, 0)
        stride = 8

        def second(g, carry):
            rows = conv(one_layer, w_pair, w_one, bias_two, 1, base + g * stride, stride)
            for a in range(3):
                grown[pl.ds(g * stride, stride), a] = (
                    rows[a].astype(BF).reshape(stride, ROWS, LANES)
                )
            return carry

        lax.fori_loop(0, SPAN // stride, second, 0)

        pieces = []
        high = jnp.where(low_lanes, 0.0, 1.0).astype(BF)
        low = jnp.where(low_lanes, 1.0, 0.0).astype(BF)
        for p in range(16):
            skip = [
                one_layer[base + t * 16 + p + 1, 1:4] * low
                + one_layer[base + t * 16 + p, 1:4] * high
                for t in range(2)
            ]
            made = [grown[t * 16 + p] for t in range(2)]
            for part in (made, skip):
                pieces.append(jnp.concatenate([v.reshape(3 * ROWS, LANES) for v in part], axis=0))
        fields = dot(jnp.concatenate(pieces, axis=1), w_head[...].reshape(16 * 256, LANES))
        fields = (fields + bias_head).astype(BF)
        outgoing[c] = dot(spread[...], fields).astype(BF).reshape(lat_count, SUB, LANES)

        def send(t, carry):
            target = (me + t) % lat_count
            pltpu.make_async_remote_copy(
                src_ref=outgoing.at[c, target],
                dst_ref=incoming.at[c, me],
                send_sem=out_send.at[c],
                recv_sem=out_recv.at[c],
                device_id={"lat": target, "lon": lon},
                device_id_type=MESH,
            ).start()
            return carry

        lax.fori_loop(1, lat_count, send, 0)
        incoming[c, me] = outgoing[c, me]
        return carry

    lax.fori_loop(0, CHUNKS, chunk, 0)

    for c in range(CHUNKS):
        rest = pl.ds(0, lat_count - 1)
        pltpu.make_async_copy(incoming.at[c, rest], incoming.at[c, rest], out_recv.at[c]).wait()
        landed = incoming[c].reshape(lat_count * SUB, LANES)
        made = dot(gather[...], landed)
        for t in range(2):
            block = made[t * slots * 4 : (t + 1) * slots * 4].reshape(slots, 4, LANES)
            at = (2 * c + t) * LANES
            out_ref[:, :, at : at + LANES] = block[:, 0:3]
    for c in range(CHUNKS):
        rest = pl.ds(0, lat_count - 1)
        pltpu.make_async_copy(outgoing.at[c, rest], outgoing.at[c, rest], out_send.at[c]).wait()


def body(lat_count, lon_count, coarse, ocean_mask, band_plan, up_weight, up_bias, first_weight,
         first_bias, second_weight, second_bias, head_weight, head_bias):
    slots = 32
    vmem = pl.BlockSpec(memory_space=pltpu.VMEM)
    row = lambda v: v.reshape(1, -1)
    return pl.pallas_call(
        partial(kernel, lat_count, lon_count),
        out_shape=jax.ShapeDtypeStruct((slots, 3, 768), F32),
        in_specs=[vmem] * 11,
        out_specs=vmem,
        scratch_shapes=[
            pltpu.VMEM((2, 1, coarse.shape[1]), F32),
            pltpu.VMEM((2, 1, coarse.shape[1]), F32),
            pltpu.VMEM((2, 2, 1, LANES), F32),
            pltpu.VMEM((2, ROWS, LANES), BF),
            pltpu.VMEM((PAIRS, ROWS, LANES), BF),
            pltpu.VMEM((3 * PAIRS + 2, 5, ROWS, LANES), BF),
            pltpu.VMEM((3 * PAIRS + 1, 5, ROWS, LANES), BF),
            pltpu.VMEM((SPAN, 3, ROWS, LANES), BF),
            pltpu.VMEM((3, LANES, 3 * LANES), BF),
            pltpu.VMEM((2, 1024, 2 * LANES), BF),
            pltpu.VMEM((2, 768, LANES), BF),
            pltpu.VMEM((16, 256, LANES), BF),
            pltpu.VMEM((2, ROWS, LANES), BF),
            pltpu.VMEM((lat_count * SUB, 6 * ROWS), BF),
            pltpu.VMEM((2 * slots * 4, lat_count * SUB), BF),
            pltpu.VMEM((CHUNKS, lat_count, SUB, LANES), BF),
            pltpu.VMEM((CHUNKS, lat_count, SUB, LANES), BF),
            pltpu.SemaphoreType.DMA((8,)),
            pltpu.SemaphoreType.DMA((8,)),
            pltpu.SemaphoreType.DMA((CHUNKS,)),
            pltpu.SemaphoreType.DMA((CHUNKS,)),
        ],
        compiler_params=pltpu.CompilerParams(
            collective_id=0, has_side_effects=True, vmem_limit_bytes=60 * 2**20
        ),
    )(
        coarse,
        ocean_mask.reshape(-1, LANES),
        band_plan.reshape(-1, LANES),
        up_weight,
        row(up_bias),
        first_weight,
        row(first_bias),
        second_weight,
        row(second_bias),
        head_weight,
        row(head_bias),
    )


def solution(mesh):
    in_specs = (P("lat", "lon"), P(), P(), P(), P(), P(), P(), P(), P(), P(), P())
    out_specs = P("lat", None, "lon")
    call = partial(body, mesh.shape["lat"], mesh.shape["lon"])
    return jax.shard_map(call, mesh=mesh, in_specs=in_specs, out_specs=out_specs, check_vma=False)
```

time: 411 us -> 65.3 us (0.16)
  the two profiles are of different devices: /device:TPU:25 before, /device:TPU:32 now
where the time goes in v1:
time: 65.3 us; the launch traced here: 65.1 us
  Pallas kernels  61.9 us (95%)
  local copies, waits for them, and re-layouts  3.15 us (5%)
    pallas_call x1, Pallas kernels, body(): pl.pallas_call(partial(kernel, lat_count, lon_count), out_shape=jax.Shape...  61.9 us
    pallas_call x1, local copies, waits for them, and re-layouts, body(): pl.pallas_call(partial(kernel, lat_count, lon_count), out_shape=jax.Shape...  1.77 us
    unnamed x3, local copies, waits for them, and re-layouts  1.39 us

profile of v1, /device:TPU:32, one launch (start us, length us, event | category | flops | bytes accessed | tf_op | source)
XLA Modules:
  0.0 65.1 jit_solution(6075897063686371026)
XLA Ops:
  0.0 0.0 copy-start
  0.0 0.7 %copy-done = bf16[64,4]{0,1:T(4,128)(2,1)S(1)} copy-done((bf16[64,4]{0,1:T(4,128)(2,1)S(1)}, bf16[64,4]{0,1:T(4,128)(2,1)}, u32[]{:S(2)}) %copy-start) | copy-done | bytes 536
  0.7 0.7 %copy.12.head_weight = bf16[64,4]{1,0:T(8,128)(2,1)} copy(bf16[64,4]{0,1:T(4,128)(2,1)S(1)} %copy-done) | data formatting | bytes 1024 | tf_op args[9]
  1.4 61.9 %shard_map.109 = f32[32,3,768]{2,1,0:T(4,128)} custom-call(bf16[64,4096]{1,0:T(8,128)(2,1)} %x_ref.1, s32[16,128]{1,0:T(8,128)} %bitcast.6, s32[16,128]{1,0:T(8,128)} %bitcast.7, bf16[3,3,64,64]{3,2,1,0:T(8,128)(2,1)} %up_weight.1, f32[1,64]{1,0:T(1,128)} %bitcast.8, bf16[3,3,64,64]{3,2,1,0:T(8,128)(2,1)} %first_weight.1, f32[1,64]{1,0:T(1,128)} %bitcast.9, ...), custom_call_target="tpu_custom_call" | custom-call | tf_op jit(solution)/shard_map/pallas_call | solution.py:417
  63.3 1.8 %copy.13 = f32[32,3,768]{2,0,1:T(8,128)} copy(f32[32,3,768]{2,1,0:T(4,128)} %shard_map.109) | data formatting | bytes 589824 | tf_op jit(solution)/shard_map/pallas_call | solution.py:417
Async XLA Ops:
  0.0 0.7 %copy-start = (bf16[64,4]{0,1:T(4,128)(2,1)S(1)}, bf16[64,4]{0,1:T(4,128)(2,1)}, u32[]{:S(2)}) copy-start(bf16[64,4]{0,1:T(4,128)(2,1)} %param.20) | copy-start | bytes 1540

commit v2 on v1

--- a/solution.py
+++ b/solution.py
@@ -12,11 +12,11 @@
 BF = jnp.bfloat16
 F32 = jnp.float32
 ROWS = 64
+SENT = 12
 SUB = 16
 TILES = ROWS // SUB
 LANES = 128
 PAIRS = 32
-GROUP = 11
 CHUNKS = 3
 SPAN = 32
 SLOPE = float(np.sqrt(2.0 / np.pi))
@@ -35,7 +35,8 @@
 
 
 def gelu_of_half(h):
-    return h + h * jnp.tanh(h * (2 * SLOPE + (8 * 0.044715 * SLOPE) * (h * h)))
+    h = h.astype(BF)
+    return h + h * jnp.tanh(h * (BF(2 * SLOPE) + BF(8 * 0.044715 * SLOPE) * (h * h)))
 
 
 def place_of(m):
@@ -43,10 +44,10 @@
 
 
 def store_layer(ref, at, a, value, masks):
-    rounded = value.astype(BF)
+    rounded = value
     ref[at, a + 1] = rounded
     if a == 2:
-        rolled = pltpu.roll(value[ROWS - SUB :], 1, 0).astype(BF)
+        rolled = pltpu.roll(value[ROWS - SUB :].astype(F32), 1, 0).astype(BF)
         ref[at, 0, 0:SUB] = rolled * masks[0, 0:SUB]
         for t in range(1, TILES):
             low = t * SUB
@@ -57,7 +58,7 @@
             ref[at, 4, low : low + SUB] = (
                 rounded[low + SUB : low + 2 * SUB] * masks[1, low : low + SUB]
             )
-        rolled = pltpu.roll(value[:SUB], SUB - 1, 0).astype(BF)
+        rolled = pltpu.roll(value[:SUB].astype(F32), SUB - 1, 0).astype(BF)
         ref[at, 4, ROWS - SUB :] = rolled * masks[1, ROWS - SUB :]
 
 
@@ -80,6 +81,8 @@
 
 def build_conv(weight_ref, w_pair, w_one, layer):
     low, high = widen(weight_ref)
+    if layer == 1:
+        low, high = high, low
     zero = jnp.zeros((256, LANES), BF)
     blocks = [
         jnp.concatenate(
@@ -102,20 +105,26 @@
         first = [low[a][0] + high[a][1], low[a][2], zero]
         second = [zero, high[a][0], low[a][1] + high[a][2]]
         for n in range(3):
-            at = slice(n * LANES, (n + 1) * LANES)
-            w_up[a, 0:64, at] = first[n]
-            w_up[a, 64:128, at] = second[n]
+            at = slice((3 * a + n) * LANES, (3 * a + n + 1) * LANES)
+            w_up[0:64, at] = first[n]
+            w_up[64:128, at] = second[n]
 
 
 def build_head(weight_ref, w_head):
-    fields = weight_ref.shape[1]
+    fields = weight_ref.shape[0]
     row, lane = iota((fields, LANES), 0), iota((fields, LANES), 1)
-    tiled = dot(weight_ref[...], (lane % fields == row).astype(BF))
+    tiled = lax.dot_general(
+        weight_ref[...],
+        (lane % fields == row).astype(BF),
+        (((0,), (0,)), ((), ())),
+        preferred_element_type=F32,
+    )
     pixel = iota(tiled.shape, 1) // fields
     for p in range(16):
-        for part, v in enumerate((0, 1, 1, 0)):
+        for part, v in enumerate((1, 0)):
             block = jnp.where(pixel == 2 * p + v, tiled, 0.0).astype(BF)
-            w_head[p, part * 64 : (part + 1) * 64, :] = block
+            at = p * LANES + part * 64
+            w_head[at : at + 64, :] = block
 
 
 def conv(ref, w_pair, w_one, bias, layer, at, count):
@@ -190,6 +199,11 @@
             barrier, inc=1, device_id={"lat": r, "lon": c}, device_id_type=MESH
         )
 
+    build_up(up_weight, w_up)
+    build_conv(first_weight, w_pair, w_one, 0)
+    build_conv(second_weight, w_pair, w_one, 1)
+    build_head(head_weight, w_head)
+
     edge[0] = x_ref[0:SUB, :].astype(F32)[0:1]
     edge[1] = x_ref[ROWS - SUB :, :].astype(F32)[SUB - 1 :]
 
@@ -251,53 +265,45 @@
 
     earlier = jnp.where(band_col == band_row, before, 0.0) * ocean_col
     turn_row = jnp.sum(earlier, axis=0, keepdims=True)
-    line = iota((lat_count * SUB, ROWS), 0)
-    slot = (line // SUB * 2 + line % SUB // 6).astype(F32)
-    fits = (slot == band_row * 2.0 + turn_row) & (line % SUB < 12)
-    leaves = jnp.where(fits, ocean_row, 0.0).astype(BF)
+    line = iota((lat_count * SENT, ROWS), 0)
+    slot = (line // SENT * 2 + line % SENT // 6).astype(F32)
+    leaves = jnp.where(slot == band_row * 2.0 + turn_row, ocean_row, 0.0).astype(BF)
     lane = iota((ROWS, 6 * ROWS), 1)
     there = place_of(lane % ROWS).astype(F32) == order_col
     there = jnp.where(there, ocean_col, 0.0).astype(BF)
     moved = dot(leaves, there)
     line, lane = iota(moved.shape, 0), iota(moved.shape, 1)
-    spread[...] = jnp.where(line % SUB % 6 == lane // ROWS, moved, 0.0).astype(BF)
+    spread[...] = jnp.where(line % 6 == lane // ROWS, moved, 0.0).astype(BF)
 
     arrive = jnp.where(band_all.astype(F32) == me.astype(F32), ocean_all.astype(F32), 0.0)
-    width_in = lat_count * SUB
-    home = iota((LANES, width_in), 1) // SUB
+    width_in = lat_count * SENT
+    home = iota((LANES, width_in), 1) // SENT
     counts = dot(arrive.astype(BF), (iota((LANES, width_in), 0) // ROWS == home % 2).astype(BF))
-    home = iota(counts.shape, 1) // SUB
+    home = iota(counts.shape, 1) // SENT
     count_row = jnp.sum(
         jnp.where(iota(counts.shape, 0) == home // 2, counts, 0.0), axis=0, keepdims=True
     )
     sooner = jnp.where(iota(counts.shape, 0) < home // 2, counts, 0.0)
-    other = dot(arrive.astype(BF), (iota((LANES, width_in), 0) // ROWS != iota((LANES, width_in), 1) // SUB % 2).astype(BF))
+    other = dot(arrive.astype(BF), (iota((LANES, width_in), 0) // ROWS != iota((LANES, width_in), 1) // SENT % 2).astype(BF))
     sooner = sooner + jnp.where(iota(counts.shape, 0) < home // 2, other, 0.0)
     sooner = sooner + jnp.where(
         (iota(counts.shape, 0) == home // 2) & (home % 2 == 1), other, 0.0
     )
     base_row = jnp.sum(sooner, axis=0, keepdims=True)
-    slots = out_ref.shape[0]
-    shape = (2 * slots * 4, width_in)
+    slots = out_ref.shape[1]
+    shape = (6 * slots, width_in)
     line, lane = iota(shape, 0), iota(shape, 1)
-    turn = lane % SUB // 6
-    part = lane % SUB % 6
-    wanted = (line // (slots * 4)) * 3 + line % 4
-    number = (line // 4 % slots - turn).astype(F32)
-    hit = (number == base_row) & (turn.astype(F32) < count_row)
-    hit = hit & (part == wanted) & (line % 4 < 3) & (lane % SUB < 12)
+    turn = lane % SENT // 6
+    number = (line % slots - turn).astype(F32)
+    hit = (number == base_row) & (turn.astype(F32) < count_row) & (lane % 6 == line // slots)
     gather[...] = jnp.where(hit, 1.0, 0.0).astype(BF)
 
-    build_up(up_weight, w_up)
-    build_conv(first_weight, w_pair, w_one, 0)
-    build_conv(second_weight, w_pair, w_one, 1)
-    build_head(head_weight, w_head)
     bias_up, bias_one, bias_two = (
         jnp.concatenate([b[...], b[...]], axis=1) * 0.5 for b in (up_bias, first_bias, second_bias)
     )
     bias_head = jnp.concatenate([head_bias[...]] * (LANES // head_bias.shape[1]), axis=1)
 
-    for copy in copies:
+    for copy in copies[:2]:
         copy.wait()
 
     ends = iota((ROWS, SUB), 1)
@@ -314,68 +320,54 @@
     for j in range(PAIRS):
         xc[j] = lifted[:, j * LANES : (j + 1) * LANES]
     low_lanes = iota((1, LANES), 1) < 64
-    joined = jnp.where(low_lanes, side[0].astype(F32), side[1].astype(F32)).astype(BF)
-    joined_ends = two_rows(
-        jnp.where(low_lanes, corner[0, 0], corner[0, 1]),
-        jnp.where(low_lanes, corner[1, 0], corner[1, 1]),
-    )
-    outer = dot(pick_all, jnp.concatenate([joined, joined_ends], axis=0)).astype(BF)
-    for a in range(3):
-        z = dot(outer, w_up[a])
-        for n, at in ((2, 0), (0, 3 * PAIRS + 1)):
-            grow = gelu_of_half(z[:, n * LANES : (n + 1) * LANES] + bias_up)
-            store_layer(zero_layer, at, a, grow, masks)
-
-    def chunk(c, carry):
-        start = jnp.minimum(c * GROUP, PAIRS - GROUP)
-        source = xc[pl.ds(start, GROUP)].reshape(GROUP * ROWS, LANES)
+
+    def outer_columns():
+        for copy in copies[2:]:
+            copy.wait()
+        joined = jnp.where(low_lanes, side[0].astype(F32), side[1].astype(F32)).astype(BF)
+        joined_ends = two_rows(
+            jnp.where(low_lanes, corner[0, 0], corner[0, 1]),
+            jnp.where(low_lanes, corner[1, 0], corner[1, 1]),
+        )
+        outer = dot(pick_all, jnp.concatenate([joined, joined_ends], axis=0)).astype(BF)
+        z = dot(outer, w_up[...])
         for a in range(3):
-            z = dot(source, w_up[a])
+            for n, at in ((2, 0), (0, 3 * PAIRS + 1)):
+                grow = gelu_of_half(z[:, (3 * a + n) * LANES :][:, :LANES] + bias_up)
+                store_layer(zero_layer, at, a, grow, masks)
+
+    def chunk(c, start, group):
+        source = xc[pl.ds(start, group)].reshape(group * ROWS, LANES)
+        z = dot(source, w_up[...])
+        for a in range(3):
             for n in range(3):
-                grow = gelu_of_half(z[:, n * LANES : (n + 1) * LANES] + bias_up)
-                for j in range(GROUP):
+                grow = gelu_of_half(z[:, (3 * a + n) * LANES :][:, :LANES] + bias_up)
+                for j in range(group):
                     value = grow[j * ROWS : (j + 1) * ROWS]
                     store_layer(zero_layer, 3 * (start + j) + 1 + n, a, value, masks)
 
         base = c * SPAN
-        step = 11
-
-        def first(g, carry):
-            at = base + g * step
-            rows = conv(zero_layer, w_pair, w_one, bias_one, 0, at, step)
-            for a in range(3):
-                for j in range(step):
-                    store_layer(one_layer, at + j, a, rows[a][j * ROWS : (j + 1) * ROWS], masks)
-            return carry
-
-        lax.fori_loop(0, (SPAN + 1) // step, first, 0)
-        stride = 8
-
-        def second(g, carry):
-            rows = conv(one_layer, w_pair, w_one, bias_two, 1, base + g * stride, stride)
-            for a in range(3):
-                grown[pl.ds(g * stride, stride), a] = (
-                    rows[a].astype(BF).reshape(stride, ROWS, LANES)
-                )
-            return carry
-
-        lax.fori_loop(0, SPAN // stride, second, 0)
-
-        pieces = []
+        count = SPAN + 1
+        rows = conv(zero_layer, w_pair, w_one, bias_one, 0, base, count)
+        for a in range(3):
+            for j in range(count):
+                store_layer(one_layer, base + j, a, rows[a][j * ROWS : (j + 1) * ROWS], masks)
+
+        rows = conv(one_layer, w_pair, w_one, bias_two, 1, base, SPAN)
         high = jnp.where(low_lanes, 0.0, 1.0).astype(BF)
         low = jnp.where(low_lanes, 1.0, 0.0).astype(BF)
+        for a in range(3):
+            for j in range(SPAN):
+                skip = one_layer[base + j + 1, a + 1] * low + one_layer[base + j, a + 1] * high
+                grown[j, a] = rows[a][j * ROWS : (j + 1) * ROWS] + skip
+
+        pieces = []
         for p in range(16):
-            skip = [
-                one_layer[base + t * 16 + p + 1, 1:4] * low
-                + one_layer[base + t * 16 + p, 1:4] * high
-                for t in range(2)
-            ]
-            made = [grown[t * 16 + p] for t in range(2)]
-            for part in (made, skip):
-                pieces.append(jnp.concatenate([v.reshape(3 * ROWS, LANES) for v in part], axis=0))
-        fields = dot(jnp.concatenate(pieces, axis=1), w_head[...].reshape(16 * 256, LANES))
+            made = [grown[t * 16 + p].reshape(3 * ROWS, LANES) for t in range(2)]
+            pieces.append(jnp.concatenate(made, axis=0))
+        fields = dot(jnp.concatenate(pieces, axis=1), w_head[...])
         fields = (fields + bias_head).astype(BF)
-        outgoing[c] = dot(spread[...], fields).astype(BF).reshape(lat_count, SUB, LANES)
+        outgoing[c] = dot(spread[...], fields).astype(BF).reshape(lat_count, SENT // 4, 4, LANES)
 
         def send(t, carry):
             target = (me + t) % lat_count
@@ -391,20 +383,22 @@
 
         lax.fori_loop(1, lat_count, send, 0)
         incoming[c, me] = outgoing[c, me]
-        return carry
-
-    lax.fori_loop(0, CHUNKS, chunk, 0)
-
-    for c in range(CHUNKS):
+
+    chunk(1, 10, 12)
+    outer_columns()
+    chunk(2, 22, 10)
+    chunk(0, 0, 10)
+
+    for c in (1, 2, 0):
         rest = pl.ds(0, lat_count - 1)
         pltpu.make_async_copy(incoming.at[c, rest], incoming.at[c, rest], out_recv.at[c]).wait()
-        landed = incoming[c].reshape(lat_count * SUB, LANES)
+        landed = incoming[c].reshape(lat_count * SENT, LANES)
         made = dot(gather[...], landed)
         for t in range(2):
-            block = made[t * slots * 4 : (t + 1) * slots * 4].reshape(slots, 4, LANES)
-            at = (2 * c + t) * LANES
-            out_ref[:, :, at : at + LANES] = block[:, 0:3]
-    for c in range(CHUNKS):
+            for a in range(3):
+                at = (t * 3 + a) * slots
+                out_ref[a, :, pl.ds((2 * c + t) * LANES, LANES)] = made[at : at + slots]
+    for c in (1, 2, 0):
         rest = pl.ds(0, lat_count - 1)
         pltpu.make_async_copy(outgoing.at[c, rest], outgoing.at[c, rest], out_send.at[c]).wait()
 
@@ -414,9 +408,9 @@
     slots = 32
     vmem = pl.BlockSpec(memory_space=pltpu.VMEM)
     row = lambda v: v.reshape(1, -1)
-    return pl.pallas_call(
+    made = pl.pallas_call(
         partial(kernel, lat_count, lon_count),
-        out_shape=jax.ShapeDtypeStruct((slots, 3, 768), F32),
+        out_shape=jax.ShapeDtypeStruct((3, slots, 768), F32),
         in_specs=[vmem] * 11,
         out_specs=vmem,
         scratch_shapes=[
@@ -428,15 +422,15 @@
             pltpu.VMEM((3 * PAIRS + 2, 5, ROWS, LANES), BF),
             pltpu.VMEM((3 * PAIRS + 1, 5, ROWS, LANES), BF),
             pltpu.VMEM((SPAN, 3, ROWS, LANES), BF),
-            pltpu.VMEM((3, LANES, 3 * LANES), BF),
+            pltpu.VMEM((LANES, 9 * LANES), BF),
             pltpu.VMEM((2, 1024, 2 * LANES), BF),
             pltpu.VMEM((2, 768, LANES), BF),
-            pltpu.VMEM((16, 256, LANES), BF),
+            pltpu.VMEM((16 * LANES, LANES), BF),
             pltpu.VMEM((2, ROWS, LANES), BF),
-            pltpu.VMEM((lat_count * SUB, 6 * ROWS), BF),
-            pltpu.VMEM((2 * slots * 4, lat_count * SUB), BF),
-            pltpu.VMEM((CHUNKS, lat_count, SUB, LANES), BF),
-            pltpu.VMEM((CHUNKS, lat_count, SUB, LANES), BF),
+            pltpu.VMEM((lat_count * SENT, 6 * ROWS), BF),
+            pltpu.VMEM((6 * slots, lat_count * SENT), BF),
+            pltpu.VMEM((CHUNKS, lat_count, SENT // 4, 4, LANES), BF),
+            pltpu.VMEM((CHUNKS, lat_count, SENT // 4, 4, LANES), BF),
             pltpu.SemaphoreType.DMA((8,)),
             pltpu.SemaphoreType.DMA((8,)),
             pltpu.SemaphoreType.DMA((CHUNKS,)),
@@ -455,9 +449,10 @@
         row(first_bias),
         second_weight,
         row(second_bias),
-        head_weight,
+        head_weight.T,
         row(head_bias),
     )
+    return made.transpose(1, 0, 2)
 
 
 def solution(mesh):

time: 65.3 us -> 55.7 us (0.85)
  the two profiles are of different devices: /device:TPU:32 before, /device:TPU:2 now
where the time goes in v2:
time: 55.7 us; the launch traced here: 55.6 us
  Pallas kernels  53.9 us (97%)
  local copies, waits for them, and re-layouts  1.69 us (3%)
    pallas_call x1, Pallas kernels, body(): pl.pallas_call(partial(kernel, lat_count, lon_count), out_shape=jax.Shape...  53.9 us
    unnamed x1, local copies, waits for them, and re-layouts  1.69 us

profile of v2, /device:TPU:2, one launch (start us, length us, event | category | flops | bytes accessed | tf_op | source)
XLA Modules:
  0.0 55.6 jit_solution(6346145057233291302)
XLA Ops:
  0.0 53.9 %shard_map.109 = f32[3,32,768]{2,1,0:T(8,128)} custom-call(bf16[64,4096]{1,0:T(8,128)(2,1)} %x_ref.1, s32[16,128]{1,0:T(8,128)} %bitcast.9, s32[16,128]{1,0:T(8,128)} %bitcast.10, bf16[3,3,64,64]{3,2,1,0:T(8,128)(2,1)} %up_weight.1, f32[1,64]{1,0:T(1,128)} %bitcast.12, bf16[3,3,64,64]{3,2,1,0:T(8,128)(2,1)} %first_weight.1, f32[1,64]{1,0:T(1,128)} %bitcast.13, ...), custom_call_target="tpu_custom_call" | custom-call | tf_op jit(solution)/shard_map/pallas_call | solution.py:411
  53.9 1.7 %copy.13 = f32[32,3,768]{2,0,1:T(8,128)} copy(f32[32,3,768]{2,0,1:T(8,128)} %bitcast.8) | data formatting | bytes 589824

commit v3 on v2

--- a/solution.py
+++ b/solution.py
@@ -12,13 +12,14 @@
 BF = jnp.bfloat16
 F32 = jnp.float32
 ROWS = 64
-SENT = 12
+SENT = 6
+MOST = 2
+WIDE = 16
 SUB = 16
 TILES = ROWS // SUB
 LANES = 128
 PAIRS = 32
-CHUNKS = 3
-SPAN = 32
+PARTS = ((2, 3), (0, 2), (5, 1))
 SLOPE = float(np.sqrt(2.0 / np.pi))
 
 
@@ -266,14 +267,14 @@
     earlier = jnp.where(band_col == band_row, before, 0.0) * ocean_col
     turn_row = jnp.sum(earlier, axis=0, keepdims=True)
     line = iota((lat_count * SENT, ROWS), 0)
-    slot = (line // SENT * 2 + line % SENT // 6).astype(F32)
+    slot = (line // SENT * MOST + line % MOST).astype(F32)
     leaves = jnp.where(slot == band_row * 2.0 + turn_row, ocean_row, 0.0).astype(BF)
-    lane = iota((ROWS, 6 * ROWS), 1)
+    lane = iota((ROWS, 3 * ROWS), 1)
     there = place_of(lane % ROWS).astype(F32) == order_col
     there = jnp.where(there, ocean_col, 0.0).astype(BF)
     moved = dot(leaves, there)
     line, lane = iota(moved.shape, 0), iota(moved.shape, 1)
-    spread[...] = jnp.where(line % 6 == lane // ROWS, moved, 0.0).astype(BF)
+    spread[...] = jnp.where(line % SENT // MOST == lane // ROWS, moved, 0.0).astype(BF)
 
     arrive = jnp.where(band_all.astype(F32) == me.astype(F32), ocean_all.astype(F32), 0.0)
     width_in = lat_count * SENT
@@ -291,11 +292,11 @@
     )
     base_row = jnp.sum(sooner, axis=0, keepdims=True)
     slots = out_ref.shape[1]
-    shape = (6 * slots, width_in)
+    shape = (3 * slots, width_in)
     line, lane = iota(shape, 0), iota(shape, 1)
-    turn = lane % SENT // 6
+    turn = lane % MOST
     number = (line % slots - turn).astype(F32)
-    hit = (number == base_row) & (turn.astype(F32) < count_row) & (lane % 6 == line // slots)
+    hit = (number == base_row) & (turn.astype(F32) < count_row) & (lane % SENT // MOST == line // slots)
     gather[...] = jnp.where(hit, 1.0, 0.0).astype(BF)
 
     bias_up, bias_one, bias_two = (
@@ -304,7 +305,7 @@
     bias_head = jnp.concatenate([head_bias[...]] * (LANES // head_bias.shape[1]), axis=1)
 
     for copy in copies[:2]:
-        copy.wait()
+        copy.wait_recv()
 
     ends = iota((ROWS, SUB), 1)
     pick_ends = jnp.where(ends == 0, top, jnp.where(ends == 1, bottom, 0.0))
@@ -323,7 +324,7 @@
 
     def outer_columns():
         for copy in copies[2:]:
-            copy.wait()
+            copy.wait_recv()
         joined = jnp.where(low_lanes, side[0].astype(F32), side[1].astype(F32)).astype(BF)
         joined_ends = two_rows(
             jnp.where(low_lanes, corner[0, 0], corner[0, 1]),
@@ -336,7 +337,10 @@
                 grow = gelu_of_half(z[:, (3 * a + n) * LANES :][:, :LANES] + bias_up)
                 store_layer(zero_layer, at, a, grow, masks)
 
-    def chunk(c, start, group):
+    high = jnp.where(low_lanes, 0.0, 1.0).astype(BF)
+    low = jnp.where(low_lanes, 1.0, 0.0).astype(BF)
+
+    def lift(start, group):
         source = xc[pl.ds(start, group)].reshape(group * ROWS, LANES)
         z = dot(source, w_up[...])
         for a in range(3):
@@ -346,61 +350,73 @@
                     value = grow[j * ROWS : (j + 1) * ROWS]
                     store_layer(zero_layer, 3 * (start + j) + 1 + n, a, value, masks)
 
-        base = c * SPAN
-        count = SPAN + 1
+    def convolve(base, count):
         rows = conv(zero_layer, w_pair, w_one, bias_one, 0, base, count)
         for a in range(3):
             for j in range(count):
                 store_layer(one_layer, base + j, a, rows[a][j * ROWS : (j + 1) * ROWS], masks)
 
-        rows = conv(one_layer, w_pair, w_one, bias_two, 1, base, SPAN)
-        high = jnp.where(low_lanes, 0.0, 1.0).astype(BF)
-        low = jnp.where(low_lanes, 1.0, 0.0).astype(BF)
+    def finish(n):
+        tile, tiles = PARTS[n]
+        base = tile * WIDE
+        rows = conv(one_layer, w_pair, w_one, bias_two, 1, base, tiles * WIDE)
         for a in range(3):
-            for j in range(SPAN):
+            for j in range(tiles * WIDE):
                 skip = one_layer[base + j + 1, a + 1] * low + one_layer[base + j, a + 1] * high
                 grown[j, a] = rows[a][j * ROWS : (j + 1) * ROWS] + skip
 
         pieces = []
-        for p in range(16):
-            made = [grown[t * 16 + p].reshape(3 * ROWS, LANES) for t in range(2)]
+        for p in range(WIDE):
+            made = [grown[i * WIDE + p].reshape(3 * ROWS, LANES) for i in range(tiles)]
             pieces.append(jnp.concatenate(made, axis=0))
         fields = dot(jnp.concatenate(pieces, axis=1), w_head[...])
         fields = (fields + bias_head).astype(BF)
-        outgoing[c] = dot(spread[...], fields).astype(BF).reshape(lat_count, SENT // 4, 4, LANES)
+        for i in range(tiles):
+            sent = dot(spread[...], fields[i * 3 * ROWS : (i + 1) * 3 * ROWS]).astype(BF)
+            outgoing[tile + i] = sent.reshape(lat_count, 3, MOST, LANES)
 
         def send(t, carry):
             target = (me + t) % lat_count
             pltpu.make_async_remote_copy(
-                src_ref=outgoing.at[c, target],
-                dst_ref=incoming.at[c, me],
-                send_sem=out_send.at[c],
-                recv_sem=out_recv.at[c],
+                src_ref=outgoing.at[pl.ds(tile, tiles), target],
+                dst_ref=incoming.at[pl.ds(tile, tiles), me],
+                send_sem=out_send.at[n],
+                recv_sem=out_recv.at[n],
                 device_id={"lat": target, "lon": lon},
                 device_id_type=MESH,
             ).start()
             return carry
 
         lax.fori_loop(1, lat_count, send, 0)
-        incoming[c, me] = outgoing[c, me]
-
-    chunk(1, 10, 12)
+        for i in range(tiles):
+            incoming[tile + i, me] = outgoing[tile + i, me]
+
+    lift(10, 17)
+    convolve(32, 49)
+    finish(0)
     outer_columns()
-    chunk(2, 22, 10)
-    chunk(0, 0, 10)
-
-    for c in (1, 2, 0):
-        rest = pl.ds(0, lat_count - 1)
-        pltpu.make_async_copy(incoming.at[c, rest], incoming.at[c, rest], out_recv.at[c]).wait()
-        landed = incoming[c].reshape(lat_count * SENT, LANES)
-        made = dot(gather[...], landed)
-        for t in range(2):
+    lift(0, 10)
+    convolve(0, 32)
+    finish(1)
+    lift(27, 5)
+    convolve(81, 16)
+    finish(2)
+
+    rest = pl.ds(0, lat_count - 1)
+    for n, (tile, tiles) in enumerate(PARTS):
+        block = incoming.at[pl.ds(tile, tiles), rest]
+        pltpu.make_async_copy(block, block, out_recv.at[n]).wait()
+        for i in range(tiles):
+            landed = incoming[tile + i].reshape(lat_count * SENT, LANES)
+            made = dot(gather[...], landed)
             for a in range(3):
-                at = (t * 3 + a) * slots
-                out_ref[a, :, pl.ds((2 * c + t) * LANES, LANES)] = made[at : at + slots]
-    for c in (1, 2, 0):
-        rest = pl.ds(0, lat_count - 1)
-        pltpu.make_async_copy(outgoing.at[c, rest], outgoing.at[c, rest], out_send.at[c]).wait()
+                at = pl.ds((tile + i) * LANES, LANES)
+                out_ref[a, :, at] = made[a * slots : (a + 1) * slots].astype(BF)
+    for copy in copies:
+        copy.wait_send()
+    for n, (tile, tiles) in enumerate(PARTS):
+        block = outgoing.at[pl.ds(tile, tiles), rest]
+        pltpu.make_async_copy(block, block, out_send.at[n]).wait()
 
 
 def body(lat_count, lon_count, coarse, ocean_mask, band_plan, up_weight, up_bias, first_weight,
@@ -410,7 +426,7 @@
     row = lambda v: v.reshape(1, -1)
     made = pl.pallas_call(
         partial(kernel, lat_count, lon_count),
-        out_shape=jax.ShapeDtypeStruct((3, slots, 768), F32),
+        out_shape=jax.ShapeDtypeStruct((3, slots, 768), BF),
         in_specs=[vmem] * 11,
         out_specs=vmem,
         scratch_shapes=[
@@ -421,20 +437,20 @@
             pltpu.VMEM((PAIRS, ROWS, LANES), BF),
             pltpu.VMEM((3 * PAIRS + 2, 5, ROWS, LANES), BF),
             pltpu.VMEM((3 * PAIRS + 1, 5, ROWS, LANES), BF),
-            pltpu.VMEM((SPAN, 3, ROWS, LANES), BF),
+            pltpu.VMEM((3 * WIDE, 3, ROWS, LANES), BF),
             pltpu.VMEM((LANES, 9 * LANES), BF),
             pltpu.VMEM((2, 1024, 2 * LANES), BF),
             pltpu.VMEM((2, 768, LANES), BF),
             pltpu.VMEM((16 * LANES, LANES), BF),
             pltpu.VMEM((2, ROWS, LANES), BF),
-            pltpu.VMEM((lat_count * SENT, 6 * ROWS), BF),
-            pltpu.VMEM((6 * slots, lat_count * SENT), BF),
-            pltpu.VMEM((CHUNKS, lat_count, SENT // 4, 4, LANES), BF),
-            pltpu.VMEM((CHUNKS, lat_count, SENT // 4, 4, LANES), BF),
+            pltpu.VMEM((lat_count * SENT, 3 * ROWS), BF),
+            pltpu.VMEM((3 * slots, lat_count * SENT), BF),
+            pltpu.VMEM((6, lat_count, 3, MOST, LANES), BF),
+            pltpu.VMEM((6, lat_count, 3, MOST, LANES), BF),
             pltpu.SemaphoreType.DMA((8,)),
             pltpu.SemaphoreType.DMA((8,)),
-            pltpu.SemaphoreType.DMA((CHUNKS,)),
-            pltpu.SemaphoreType.DMA((CHUNKS,)),
+            pltpu.SemaphoreType.DMA((len(PARTS),)),
+            pltpu.SemaphoreType.DMA((len(PARTS),)),
         ],
         compiler_params=pltpu.CompilerParams(
             collective_id=0, has_side_effects=True, vmem_limit_bytes=60 * 2**20
@@ -452,7 +468,7 @@
         head_weight.T,
         row(head_bias),
     )
-    return made.transpose(1, 0, 2)
+    return made.transpose(1, 0, 2).astype(F32)
 
 
 def solution(mesh):

time: 55.7 us -> 55.1 us (0.989)
  local copies, waits for them, and re-layouts: 1.69 us -> 0 us
  other arithmetic: 0 us -> 1.64 us
  Pallas kernels: 53.9 us -> 53.3 us
    unnamed x1 -> x0, local copies, waits for them, and re-layouts: 1.69 us -> none
    convert_element_type x0 -> x1, other arithmetic: none -> 1.64 us  [body(): return made.transpose(1, 0, 2).astype(F32)]
where the time goes in v3:
time: 55.1 us; the launch traced here: 55 us
  Pallas kernels  53.3 us (97%)
  other arithmetic  1.64 us (3%)
    pallas_call x1, Pallas kernels, body(): pl.pallas_call(partial(kernel, lat_count, lon_count), out_shape=jax.Shape...  53.3 us
    convert_element_type x1, other arithmetic, body(): return made.transpose(1, 0, 2).astype(F32)  1.64 us

profile of v3, /device:TPU:2, one launch (start us, length us, event | category | flops | bytes accessed | tf_op | source)
XLA Modules:
  0.0 55.0 jit_solution(4268948711880536602)
XLA Ops:
  0.0 53.3 %shard_map.109 = bf16[3,32,768]{2,1,0:T(8,128)(2,1)} custom-call(bf16[64,4096]{1,0:T(8,128)(2,1)} %x_ref.1, s32[16,128]{1,0:T(8,128)} %bitcast.9, s32[16,128]{1,0:T(8,128)} %bitcast.10, bf16[3,3,64,64]{3,2,1,0:T(8,128)(2,1)} %up_weight.1, f32[1,64]{1,0:T(1,128)} %bitcast.12, bf16[3,3,64,64]{3,2,1,0:T(8,128)(2,1)} %first_weight.1, f32[1,64]{1,0:T(1,128)} %bitcast.13, ...), custom_call_target="tpu_custom_call" | custom-call | tf_op jit(solution)/shard_map/pallas_call | solution.py:427
  53.3 1.6 %convert_bitcast_fusion = f32[32,3,768]{2,0,1:T(8,128)} fusion(bf16[3,32,768]{2,1,0:T(8,128)(2,1)} %shard_map.109), kind=kLoop, calls=%fused_computation | loop fusion | flops 73728 | bytes 442368 | tf_op jit(solution)/shard_map/convert_element_type | solution.py:471

commit v4 on v3

--- a/solution.py
+++ b/solution.py
@@ -19,7 +19,7 @@
 TILES = ROWS // SUB
 LANES = 128
 PAIRS = 32
-PARTS = ((2, 3), (0, 2), (5, 1))
+RING = 4
 SLOPE = float(np.sqrt(2.0 / np.pi))
 
 
@@ -128,106 +128,48 @@
             w_head[at : at + 64, :] = block
 
 
-def conv(ref, w_pair, w_one, bias, layer, at, count):
-    pieces = [
-        [ref[pl.ds(at + d, count), i].reshape(count * ROWS, LANES) for d in range(2)]
-        for i in range(5)
-    ]
+def conv(ref, w_pair, w_one, bias, layer, places):
+    def stack(i, d):
+        if isinstance(places, range):
+            return ref[places.start + d : places.stop + d, i].reshape(len(places) * ROWS, LANES)
+        return jnp.concatenate([ref[at + d, i] for at in places], axis=0)
+
+    pieces = [[stack(i, d) for d in range(2)] for i in range(5)]
     both = dot(jnp.concatenate(sum(pieces[:4], []), axis=1), w_pair[layer])
     last = dot(jnp.concatenate(sum(pieces[2:], []), axis=1), w_one[layer])
     rows = [both[:, :LANES], both[:, LANES:], last]
     return [gelu_of_half(z + bias) for z in rows]
 
 
-def kernel(
-    lat_count,
-    lon_count,
-    x_ref,
-    ocean_ref,
-    band_ref,
-    up_weight,
-    up_bias,
-    first_weight,
-    first_bias,
-    second_weight,
-    second_bias,
-    head_weight,
-    head_bias,
-    out_ref,
-    edge,
-    halo,
-    corner,
-    side,
-    xc,
-    zero_layer,
-    one_layer,
-    grown,
-    w_up,
-    w_pair,
-    w_one,
-    w_head,
-    masks,
-    spread,
-    gather,
-    outgoing,
-    incoming,
-    halo_send,
-    halo_recv,
-    out_send,
-    out_recv,
+def prepare(
+    lat_count, x_hbm, ocean_ref, band_ref, ends_ref, pick_out, masks, spread, gather,
+    rows, edge, halo, load, halo_send, halo_recv,
 ):
     me = lax.axis_index("lat")
     lon = lax.axis_index("lon")
     north, south = (me + lat_count - 1) % lat_count, (me + 1) % lat_count
-    west, east = (lon + lon_count - 1) % lon_count, (lon + 1) % lon_count
-    width = x_ref.shape[1]
-
     barrier = pltpu.get_barrier_semaphore()
-
-    def greet(t, carry):
-        pl.semaphore_signal(
-            barrier,
-            inc=1,
-            device_id={"lat": (me + t) % lat_count, "lon": lon},
-            device_id_type=MESH,
-        )
-        return carry
-
-    lax.fori_loop(1, lat_count, greet, 0)
-    others = [(me, west), (me, east)] + [(r, c) for r in (north, south) for c in (west, east)]
-    for r, c in others:
-        pl.semaphore_signal(
-            barrier, inc=1, device_id={"lat": r, "lon": c}, device_id_type=MESH
-        )
-
-    build_up(up_weight, w_up)
-    build_conv(first_weight, w_pair, w_one, 0)
-    build_conv(second_weight, w_pair, w_one, 1)
-    build_head(head_weight, w_head)
-
-    edge[0] = x_ref[0:SUB, :].astype(F32)[0:1]
-    edge[1] = x_ref[ROWS - SUB :, :].astype(F32)[SUB - 1 :]
-
-    pl.semaphore_wait(barrier, lat_count - 1 + len(others))
-    first, final = pl.ds(0, LANES), pl.ds(width - LANES, LANES)
-    plan = [
-        (edge.at[0], halo.at[1], north, lon),
-        (edge.at[1], halo.at[0], south, lon),
-        (x_ref.at[:, first], side.at[0], me, west),
-        (x_ref.at[:, final], side.at[1], me, east),
-        (edge.at[0, :, first], corner.at[1, 0], north, west),
-        (edge.at[0, :, final], corner.at[1, 1], north, east),
-        (edge.at[1, :, first], corner.at[0, 0], south, west),
-        (edge.at[1, :, final], corner.at[0, 1], south, east),
+    for r in (north, south):
+        pl.semaphore_signal(barrier, inc=1, device_id={"lat": r, "lon": lon}, device_id_type=MESH)
+    loads = [
+        pltpu.make_async_copy(x_hbm.at[pl.ds(low, SUB), :], rows.at[n], load.at[n])
+        for n, low in enumerate((0, ROWS - SUB))
     ]
+    for copy in loads:
+        copy.start()
+    for copy in loads:
+        copy.wait()
+    edge[0] = rows[0].astype(F32)[0:1]
+    edge[1] = rows[1].astype(F32)[SUB - 1 :]
+    pl.semaphore_wait(barrier, 2)
     copies = []
-    for n, (source, target, r, c) in enumerate(plan):
+    for n, r in enumerate((north, south)):
         copy = pltpu.make_async_remote_copy(
-            src_ref=source,
-            dst_ref=target,
+            src_ref=edge.at[n],
+            dst_ref=halo.at[1 - n],
             send_sem=halo_send.at[n],
             recv_sem=halo_recv.at[n],
-            device_id={"lat": r, "lon": c},
+            device_id={"lat": r, "lon": lon},
             device_id_type=MESH,
         )
         copy.start()
@@ -291,7 +233,7 @@
         (iota(counts.shape, 0) == home // 2) & (home % 2 == 1), other, 0.0
     )
     base_row = jnp.sum(sooner, axis=0, keepdims=True)
-    slots = out_ref.shape[1]
+    slots = gather.shape[0] // 3
     shape = (3 * slots, width_in)
     line, lane = iota(shape, 0), iota(shape, 1)
     turn = lane % MOST
@@ -299,44 +241,102 @@
     hit = (number == base_row) & (turn.astype(F32) < count_row) & (lane % SENT // MOST == line // slots)
     gather[...] = jnp.where(hit, 1.0, 0.0).astype(BF)
 
+    ends = iota((ROWS, SUB), 1)
+    pick_ends = jnp.where(ends == 0, top, jnp.where(ends == 1, bottom, 0.0))
+    pick_out[...] = jnp.concatenate([pick.astype(BF), pick_ends.astype(BF)], axis=1)
+
+    for copy in copies:
+        copy.wait_recv()
+    ends_ref[...] = halo[...]
+    for copy in copies:
+        copy.wait_send()
+
+
+def kernel(
+    lat_count,
+    lon_count,
+    x_ref,
+    ends_ref,
+    pick_ref,
+    masks,
+    spread,
+    gather,
+    up_weight,
+    up_bias,
+    first_weight,
+    first_bias,
+    second_weight,
+    second_bias,
+    head_weight,
+    head_bias,
+    out_ref,
+    edge,
+    corner,
+    side,
+    xc,
+    zero_layer,
+    one_layer,
+    grown,
+    w_up,
+    w_pair,
+    w_one,
+    w_head,
+    outgoing,
+    incoming,
+    halo_send,
+    halo_recv,
+    out_send,
+    out_recv,
+):
+    me = lax.axis_index("lat")
+    lon = lax.axis_index("lon")
+    north, south = (me + lat_count - 1) % lat_count, (me + 1) % lat_count
+    west, east = (lon + lon_count - 1) % lon_count, (lon + 1) % lon_count
+    width = x_ref.shape[1]
+    slots = out_ref.shape[1]
+
+    barrier = pltpu.get_barrier_semaphore()
+    others = [(me, west), (me, east)] + [(r, c) for r in (north, south) for c in (west, east)]
+    for r, c in others:
+        pl.semaphore_signal(
+            barrier, inc=1, device_id={"lat": r, "lon": c}, device_id_type=MESH
+        )
+
+    def greet(t, carry):
+        pl.semaphore_signal(
+            barrier,
+            inc=1,
+            device_id={"lat": (me + t) % lat_count, "lon": lon},
+            device_id_type=MESH,
+        )
+        return carry
+
+    lax.fori_loop(1, lat_count, greet, 0)
+
+    build_up(up_weight, w_up)
+    build_conv(first_weight, w_pair, w_one, 0)
+    build_conv(second_weight, w_pair, w_one, 1)
+    build_head(head_weight, w_head)
     bias_up, bias_one, bias_two = (
         jnp.concatenate([b[...], b[...]], axis=1) * 0.5 for b in (up_bias, first_bias, second_bias)
     )
     bias_head = jnp.concatenate([head_bias[...]] * (LANES // head_bias.shape[1]), axis=1)
 
-    for copy in copies[:2]:
-        copy.wait_recv()
-
-    ends = iota((ROWS, SUB), 1)
-    pick_ends = jnp.where(ends == 0, top, jnp.where(ends == 1, bottom, 0.0))
-    pick_all = jnp.concatenate([pick.astype(BF), pick_ends.astype(BF)], axis=1)
+    edge[0] = x_ref[0:SUB, :].astype(F32)[0:1]
+    edge[1] = x_ref[ROWS - SUB :, :].astype(F32)[SUB - 1 :]
+
+    pick_all = pick_ref[...]
 
     def two_rows(upper, lower):
         which = iota((SUB, upper.shape[1]), 0)
         return jnp.where(which == 0, upper, jnp.where(which == 1, lower, 0.0)).astype(BF)
 
     lifted = dot(
-        pick_all, jnp.concatenate([x_ref[...], two_rows(halo[0], halo[1])], axis=0)
+        pick_all, jnp.concatenate([x_ref[...], two_rows(ends_ref[0], ends_ref[1])], axis=0)
     ).astype(BF)
     for j in range(PAIRS):
         xc[j] = lifted[:, j * LANES : (j + 1) * LANES]
     low_lanes = iota((1, LANES), 1) < 64
-
-    def outer_columns():
-        for copy in copies[2:]:
-            copy.wait_recv()
-        joined = jnp.where(low_lanes, side[0].astype(F32), side[1].astype(F32)).astype(BF)
-        joined_ends = two_rows(
-            jnp.where(low_lanes, corner[0, 0], corner[0, 1]),
-            jnp.where(low_lanes, corner[1, 0], corner[1, 1]),
-        )
-        outer = dot(pick_all, jnp.concatenate([joined, joined_ends], axis=0)).astype(BF)
-        z = dot(outer, w_up[...])
-        for a in range(3):
-            for n, at in ((2, 0), (0, 3 * PAIRS + 1)):
-                grow = gelu_of_half(z[:, (3 * a + n) * LANES :][:, :LANES] + bias_up)
-                store_layer(zero_layer, at, a, grow, masks)
-
     high = jnp.where(low_lanes, 0.0, 1.0).astype(BF)
     low = jnp.where(low_lanes, 1.0, 0.0).astype(BF)
 
@@ -350,88 +350,143 @@
                     value = grow[j * ROWS : (j + 1) * ROWS]
                     store_layer(zero_layer, 3 * (start + j) + 1 + n, a, value, masks)
 
-    def convolve(base, count):
-        rows = conv(zero_layer, w_pair, w_one, bias_one, 0, base, count)
+    lift(0, PAIRS // 2)
+
+    pl.semaphore_wait(barrier, lat_count - 1 + len(others))
+    first, final = pl.ds(0, LANES), pl.ds(width - LANES, LANES)
+    plan = [
+        (x_ref.at[:, first], side.at[0], me, west),
+        (x_ref.at[:, final], side.at[1], me, east),
+        (edge.at[0, :, first], corner.at[1, 0], north, west),
+        (edge.at[0, :, final], corner.at[1, 1], north, east),
+        (edge.at[1, :, first], corner.at[0, 0], south, west),
+        (edge.at[1, :, final], corner.at[0, 1], south, east),
+    ]
+    copies = []
+    for n, (source, target, r, c) in enumerate(plan):
+        copy = pltpu.make_async_remote_copy(
+            src_ref=source,
+            dst_ref=target,
+            send_sem=halo_send.at[n],
+            recv_sem=halo_recv.at[n],
+            device_id={"lat": r, "lon": c},
+            device_id_type=MESH,
+        )
+        copy.start()
+        copies.append(copy)
+
+    def convolve(places):
+        rows = conv(zero_layer, w_pair, w_one, bias_one, 0, places)
         for a in range(3):
-            for j in range(count):
-                store_layer(one_layer, base + j, a, rows[a][j * ROWS : (j + 1) * ROWS], masks)
-
-    def finish(n):
-        tile, tiles = PARTS[n]
-        base = tile * WIDE
-        rows = conv(one_layer, w_pair, w_one, bias_two, 1, base, tiles * WIDE)
+            for j, at in enumerate(places):
+                store_layer(one_layer, at, a, rows[a][j * ROWS : (j + 1) * ROWS], masks)
+
+    lift(PAIRS // 2, PAIRS // 2)
+    convolve(range(1, 3 * PAIRS // 2 + 1))
+    convolve(range(3 * PAIRS // 2 + 1, 3 * PAIRS))
+
+    for copy in copies:
+        copy.wait_recv()
+    joined = jnp.where(low_lanes, side[0].astype(F32), side[1].astype(F32)).astype(BF)
+    joined_ends = two_rows(
+        jnp.where(low_lanes, corner[0, 0], corner[0, 1]),
+        jnp.where(low_lanes, corner[1, 0], corner[1, 1]),
+    )
+    outer = dot(pick_all, jnp.concatenate([joined, joined_ends], axis=0)).astype(BF)
+    z = dot(outer, w_up[...])
+    for a in range(3):
+        for n, at in ((2, 0), (0, 3 * PAIRS + 1)):
+            grow = gelu_of_half(z[:, (3 * a + n) * LANES :][:, :LANES] + bias_up)
+            store_layer(zero_layer, at, a, grow, masks)
+    convolve((0, 3 * PAIRS))
+
+    for half in range(2):
+        base = half * 3 * WIDE
+        rows = conv(one_layer, w_pair, w_one, bias_two, 1, range(base, base + 3 * WIDE))
         for a in range(3):
-            for j in range(tiles * WIDE):
+            for j in range(3 * WIDE):
                 skip = one_layer[base + j + 1, a + 1] * low + one_layer[base + j, a + 1] * high
                 grown[j, a] = rows[a][j * ROWS : (j + 1) * ROWS] + skip
-
         pieces = []
         for p in range(WIDE):
-            made = [grown[i * WIDE + p].reshape(3 * ROWS, LANES) for i in range(tiles)]
+            made = [grown[i * WIDE + p].reshape(3 * ROWS, LANES) for i in range(3)]
             pieces.append(jnp.concatenate(made, axis=0))
         fields = dot(jnp.concatenate(pieces, axis=1), w_head[...])
         fields = (fields + bias_head).astype(BF)
-        for i in range(tiles):
+        for i in range(3):
             sent = dot(spread[...], fields[i * 3 * ROWS : (i + 1) * 3 * ROWS]).astype(BF)
-            outgoing[tile + i] = sent.reshape(lat_count, 3, MOST, LANES)
-
-        def send(t, carry):
-            target = (me + t) % lat_count
-            pltpu.make_async_remote_copy(
-                src_ref=outgoing.at[pl.ds(tile, tiles), target],
-                dst_ref=incoming.at[pl.ds(tile, tiles), me],
-                send_sem=out_send.at[n],
-                recv_sem=out_recv.at[n],
-                device_id={"lat": target, "lon": lon},
-                device_id_type=MESH,
-            ).start()
-            return carry
-
-        lax.fori_loop(1, lat_count, send, 0)
-        for i in range(tiles):
-            incoming[tile + i, me] = outgoing[tile + i, me]
-
-    lift(10, 17)
-    convolve(32, 49)
-    finish(0)
-    outer_columns()
-    lift(0, 10)
-    convolve(0, 32)
-    finish(1)
-    lift(27, 5)
-    convolve(81, 16)
-    finish(2)
+            outgoing[:, half * 3 + i] = sent.reshape(lat_count, 3, MOST, LANES)
+
+    runs = lat_count // RING
+    side_of = me // RING // (runs // 2)
+
+    def send(i, carry):
+        run = i * side_of + (runs - 1 - i) * (1 - side_of)
+        for x in range(RING):
+            target = run * RING + x
+
+            @pl.when(target != me)
+            def _():
+                pltpu.make_async_remote_copy(
+                    src_ref=outgoing.at[target],
+                    dst_ref=incoming.at[me],
+                    send_sem=out_send,
+                    recv_sem=out_recv,
+                    device_id={"lat": target, "lon": lon},
+                    device_id_type=MESH,
+                ).start()
+
+        return carry
+
+    lax.fori_loop(0, runs, send, 0)
+    incoming[me] = outgoing[me]
 
     rest = pl.ds(0, lat_count - 1)
-    for n, (tile, tiles) in enumerate(PARTS):
-        block = incoming.at[pl.ds(tile, tiles), rest]
-        pltpu.make_async_copy(block, block, out_recv.at[n]).wait()
-        for i in range(tiles):
-            landed = incoming[tile + i].reshape(lat_count * SENT, LANES)
-            made = dot(gather[...], landed)
-            for a in range(3):
-                at = pl.ds((tile + i) * LANES, LANES)
-                out_ref[a, :, at] = made[a * slots : (a + 1) * slots].astype(BF)
+    pltpu.make_async_copy(incoming.at[rest], incoming.at[rest], out_recv).wait()
+    for i in range(6):
+        landed = incoming[:, i].reshape(lat_count * SENT, LANES)
+        made = dot(gather[...], landed).astype(BF)
+        for a in range(3):
+            out_ref[a, :, i * LANES : (i + 1) * LANES] = made[a * slots : (a + 1) * slots]
     for copy in copies:
         copy.wait_send()
-    for n, (tile, tiles) in enumerate(PARTS):
-        block = outgoing.at[pl.ds(tile, tiles), rest]
-        pltpu.make_async_copy(block, block, out_send.at[n]).wait()
+    pltpu.make_async_copy(outgoing.at[rest], outgoing.at[rest], out_send).wait()
 
 
 def body(lat_count, lon_count, coarse, ocean_mask, band_plan, up_weight, up_bias, first_weight,
          first_bias, second_weight, second_bias, head_weight, head_bias):
     slots = 32
+    width = coarse.shape[1]
     vmem = pl.BlockSpec(memory_space=pltpu.VMEM)
     row = lambda v: v.reshape(1, -1)
+    prepared = pl.pallas_call(
+        partial(prepare, lat_count),
+        out_shape=(
+            jax.ShapeDtypeStruct((2, 1, width), F32),
+            jax.ShapeDtypeStruct((ROWS, ROWS + SUB), BF),
+            jax.ShapeDtypeStruct((2, ROWS, LANES), BF),
+            jax.ShapeDtypeStruct((lat_count * SENT, 3 * ROWS), BF),
+            jax.ShapeDtypeStruct((3 * slots, lat_count * SENT), BF),
+        ),
+        in_specs=[pl.BlockSpec(memory_space=pl.ANY), vmem, vmem],
+        out_specs=(vmem,) * 5,
+        scratch_shapes=[
+            pltpu.VMEM((2, SUB, width), BF),
+            pltpu.VMEM((2, 1, width), F32),
+            pltpu.VMEM((2, 1, width), F32),
+            pltpu.SemaphoreType.DMA((2,)),
+            pltpu.SemaphoreType.DMA((2,)),
+            pltpu.SemaphoreType.DMA((2,)),
+        ],
+        compiler_params=pltpu.CompilerParams(collective_id=0, has_side_effects=True),
+    )(coarse, ocean_mask.reshape(-1, LANES), band_plan.reshape(-1, LANES))
     made = pl.pallas_call(
         partial(kernel, lat_count, lon_count),
         out_shape=jax.ShapeDtypeStruct((3, slots, 768), BF),
-        in_specs=[vmem] * 11,
+        in_specs=[vmem] * 14,
         out_specs=vmem,
         scratch_shapes=[
-            pltpu.VMEM((2, 1, coarse.shape[1]), F32),
-            pltpu.VMEM((2, 1, coarse.shape[1]), F32),
+            pltpu.VMEM((2, 1, width), F32),
             pltpu.VMEM((2, 2, 1, LANES), F32),
             pltpu.VMEM((2, ROWS, LANES), BF),
             pltpu.VMEM((PAIRS, ROWS, LANES), BF),
@@ -442,23 +497,19 @@
             pltpu.VMEM((2, 1024, 2 * LANES), BF),
             pltpu.VMEM((2, 768, LANES), BF),
             pltpu.VMEM((16 * LANES, LANES), BF),
-            pltpu.VMEM((2, ROWS, LANES), BF),
-            pltpu.VMEM((lat_count * SENT, 3 * ROWS), BF),
-            pltpu.VMEM((3 * slots, lat_count * SENT), BF),
-            pltpu.VMEM((6, lat_count, 3, MOST, LANES), BF),
-            pltpu.VMEM((6, lat_count, 3, MOST, LANES), BF),
-            pltpu.SemaphoreType.DMA((8,)),
-            pltpu.SemaphoreType.DMA((8,)),
-            pltpu.SemaphoreType.DMA((len(PARTS),)),
-            pltpu.SemaphoreType.DMA((len(PARTS),)),
+            pltpu.VMEM((lat_count, 6, 3, MOST, LANES), BF),
+            pltpu.VMEM((lat_count, 6, 3, MOST, LANES), BF),
+            pltpu.SemaphoreType.DMA((6,)),
+            pltpu.SemaphoreType.DMA((6,)),
+            pltpu.SemaphoreType.DMA,
+            pltpu.SemaphoreType.DMA,
         ],
         compiler_params=pltpu.CompilerParams(
-            collective_id=0, has_side_effects=True, vmem_limit_bytes=60 * 2**20
+            collective_id=1, has_side_effects=True, vmem_limit_bytes=60 * 2**20
         ),
     )(
         coarse,
-        ocean_mask.reshape(-1, LANES),
-        band_plan.reshape(-1, LANES),
+        *prepared,
         up_weight,
         row(up_bias),
         first_weight,

time: 55.1 us -> 65.2 us (1.18)
  the two profiles are of different devices: /device:TPU:2 before, /device:TPU:25 now
where the time goes in v4:
time: 65.2 us; the launch traced here: 64.9 us
  Pallas kernels  63.3 us (97%)
  other arithmetic  1.64 us (3%)
    pallas_call x1, Pallas kernels, body(): pl.pallas_call(partial(kernel, lat_count, lon_count), out_shape=jax.Shape...  45.9 us
    pallas_call x1, Pallas kernels, body(): pl.pallas_call(partial(prepare, lat_count), out_shape=(jax.ShapeDtypeStru...  17.4 us
    convert_element_type x1, other arithmetic, body(): return made.transpose(1, 0, 2).astype(F32)  1.64 us

profile of v4, /device:TPU:25, one launch (start us, length us, event | category | flops | bytes accessed | tf_op | source)
XLA Modules:
  0.0 64.9 jit_solution(14288172536802280423)
XLA Ops:
  0.0 17.4 %shard_map.109 = (f32[2,1,4096]{2,1,0:T(1,128)}, bf16[64,80]{1,0:T(8,128)(2,1)}, bf16[2,64,128]{2,1,0:T(8,128)(2,1)}, bf16[192,192]{1,0:T(8,128)(2,1)}, bf16[96,192]{1,0:T(8,128)(2,1)}) custom-call(bf16[64,4096]{1,0:T(8,128)(2,1)} %x_ref.1, s32[16,128]{1,0:T(8,128)} %bitcast.9, s32[16,128]{1,0:T(8,128)} %bitcast.10), custom_call_target="tpu_custom_call" | custom-call | tf_op jit(solution)/shard_map/pallas_call | solution.py:462
  17.4 45.9 %shard_map.110 = bf16[3,32,768]{2,1,0:T(8,128)(2,1)} custom-call(bf16[64,4096]{1,0:T(8,128)(2,1)} %x_ref.1, f32[2,1,4096]{2,1,0:T(1,128)} %get-tuple-element.10.ends_ref, bf16[64,80]{1,0:T(8,128)(2,1)} %get-tuple-element.11.pick_ref, bf16[2,64,128]{2,1,0:T(8,128)(2,1)} %get-tuple-element.12.masks, bf16[192,192]{1,0:T(8,128)(2,1)} %get-tuple-element.13.spread, ...), custom_call_target="tpu_custom_call" | custom-call | tf_op jit(solution)/shard_map/pallas_call | solution.py:483
  63.3 1.6 %convert_bitcast_fusion = f32[32,3,768]{2,0,1:T(8,128)} fusion(bf16[3,32,768]{2,1,0:T(8,128)(2,1)} %shard_map.110), kind=kLoop, calls=%fused_computation | loop fusion | flops 73728 | bytes 442368 | tf_op jit(solution)/shard_map/convert_element_type | solution.py:522

commit v5 on v3

--- a/solution.py
+++ b/solution.py
@@ -19,7 +19,6 @@
 TILES = ROWS // SUB
 LANES = 128
 PAIRS = 32
-PARTS = ((2, 3), (0, 2), (5, 1))
 SLOPE = float(np.sqrt(2.0 / np.pi))
 
 
@@ -128,9 +127,12 @@
             w_head[at : at + 64, :] = block
 
 
-def conv(ref, w_pair, w_one, bias, layer, at, count):
+def conv(ref, w_pair, w_one, bias, layer, places):
     pieces = [
-        [ref[pl.ds(at + d, count), i].reshape(count * ROWS, LANES) for d in range(2)]
+        [
+            ref[places.start + d : places.stop + d, i].reshape(len(places) * ROWS, LANES)
+            for d in range(2)
+        ]
         for i in range(5)
     ]
     both = dot(jnp.concatenate(sum(pieces[:4], []), axis=1), w_pair[layer])
@@ -181,8 +183,12 @@
     north, south = (me + lat_count - 1) % lat_count, (me + 1) % lat_count
     west, east = (lon + lon_count - 1) % lon_count, (lon + 1) % lon_count
     width = x_ref.shape[1]
-
     barrier = pltpu.get_barrier_semaphore()
+    others = [(me, west), (me, east)] + [(r, c) for r in (north, south) for c in (west, east)]
+    for r, c in others:
+        pl.semaphore_signal(
+            barrier, inc=1, device_id={"lat": r, "lon": c}, device_id_type=MESH
+        )
 
     def greet(t, carry):
         pl.semaphore_signal(
@@ -194,17 +200,11 @@
         return carry
 
     lax.fori_loop(1, lat_count, greet, 0)
-    others = [(me, west), (me, east)] + [(r, c) for r in (north, south) for c in (west, east)]
-    for r, c in others:
-        pl.semaphore_signal(
-            barrier, inc=1, device_id={"lat": r, "lon": c}, device_id_type=MESH
-        )
 
     build_up(up_weight, w_up)
     build_conv(first_weight, w_pair, w_one, 0)
     build_conv(second_weight, w_pair, w_one, 1)
     build_head(head_weight, w_head)
-
     edge[0] = x_ref[0:SUB, :].astype(F32)[0:1]
     edge[1] = x_ref[ROWS - SUB :, :].astype(F32)[SUB - 1 :]
 
@@ -321,22 +321,6 @@
     for j in range(PAIRS):
         xc[j] = lifted[:, j * LANES : (j + 1) * LANES]
     low_lanes = iota((1, LANES), 1) < 64
-
-    def outer_columns():
-        for copy in copies[2:]:
-            copy.wait_recv()
-        joined = jnp.where(low_lanes, side[0].astype(F32), side[1].astype(F32)).astype(BF)
-        joined_ends = two_rows(
-            jnp.where(low_lanes, corner[0, 0], corner[0, 1]),
-            jnp.where(low_lanes, corner[1, 0], corner[1, 1]),
-        )
-        outer = dot(pick_all, jnp.concatenate([joined, joined_ends], axis=0)).astype(BF)
-        z = dot(outer, w_up[...])
-        for a in range(3):
-            for n, at in ((2, 0), (0, 3 * PAIRS + 1)):
-                grow = gelu_of_half(z[:, (3 * a + n) * LANES :][:, :LANES] + bias_up)
-                store_layer(zero_layer, at, a, grow, masks)
-
     high = jnp.where(low_lanes, 0.0, 1.0).astype(BF)
     low = jnp.where(low_lanes, 1.0, 0.0).astype(BF)
 
@@ -350,78 +334,79 @@
                     value = grow[j * ROWS : (j + 1) * ROWS]
                     store_layer(zero_layer, 3 * (start + j) + 1 + n, a, value, masks)
 
-    def convolve(base, count):
-        rows = conv(zero_layer, w_pair, w_one, bias_one, 0, base, count)
+    lift(0, PAIRS // 2)
+    lift(PAIRS // 2, PAIRS // 2)
+
+    def convolve(places):
+        rows = conv(zero_layer, w_pair, w_one, bias_one, 0, places)
         for a in range(3):
-            for j in range(count):
-                store_layer(one_layer, base + j, a, rows[a][j * ROWS : (j + 1) * ROWS], masks)
-
-    def finish(n):
-        tile, tiles = PARTS[n]
-        base = tile * WIDE
-        rows = conv(one_layer, w_pair, w_one, bias_two, 1, base, tiles * WIDE)
+            for j, at in enumerate(places):
+                store_layer(one_layer, at, a, rows[a][j * ROWS : (j + 1) * ROWS], masks)
+
+    for copy in copies[2:]:
+        copy.wait_recv()
+    joined = jnp.where(low_lanes, side[0].astype(F32), side[1].astype(F32)).astype(BF)
+    joined_ends = two_rows(
+        jnp.where(low_lanes, corner[0, 0], corner[0, 1]),
+        jnp.where(low_lanes, corner[1, 0], corner[1, 1]),
+    )
+    outer = dot(pick_all, jnp.concatenate([joined, joined_ends], axis=0)).astype(BF)
+    z = dot(outer, w_up[...])
+    for a in range(3):
+        for n, at in ((2, 0), (0, 3 * PAIRS + 1)):
+            grow = gelu_of_half(z[:, (3 * a + n) * LANES :][:, :LANES] + bias_up)
+            store_layer(zero_layer, at, a, grow, masks)
+    convolve(range(0, 3 * WIDE + 1))
+    convolve(range(3 * WIDE + 1, 3 * PAIRS + 1))
+
+    for half in range(2):
+        base = half * 3 * WIDE
+        rows = conv(one_layer, w_pair, w_one, bias_two, 1, range(base, base + 3 * WIDE))
         for a in range(3):
-            for j in range(tiles * WIDE):
+            for j in range(3 * WIDE):
                 skip = one_layer[base + j + 1, a + 1] * low + one_layer[base + j, a + 1] * high
                 grown[j, a] = rows[a][j * ROWS : (j + 1) * ROWS] + skip
-
         pieces = []
         for p in range(WIDE):
-            made = [grown[i * WIDE + p].reshape(3 * ROWS, LANES) for i in range(tiles)]
+            made = [grown[i * WIDE + p].reshape(3 * ROWS, LANES) for i in range(3)]
             pieces.append(jnp.concatenate(made, axis=0))
         fields = dot(jnp.concatenate(pieces, axis=1), w_head[...])
         fields = (fields + bias_head).astype(BF)
-        for i in range(tiles):
+        for i in range(3):
             sent = dot(spread[...], fields[i * 3 * ROWS : (i + 1) * 3 * ROWS]).astype(BF)
-            outgoing[tile + i] = sent.reshape(lat_count, 3, MOST, LANES)
-
-        def send(t, carry):
-            target = (me + t) % lat_count
-            pltpu.make_async_remote_copy(
-                src_ref=outgoing.at[pl.ds(tile, tiles), target],
-                dst_ref=incoming.at[pl.ds(tile, tiles), me],
-                send_sem=out_send.at[n],
-                recv_sem=out_recv.at[n],
-                device_id={"lat": target, "lon": lon},
-                device_id_type=MESH,
-            ).start()
-            return carry
-
-        lax.fori_loop(1, lat_count, send, 0)
-        for i in range(tiles):
-            incoming[tile + i, me] = outgoing[tile + i, me]
-
-    lift(10, 17)
-    convolve(32, 49)
-    finish(0)
-    outer_columns()
-    lift(0, 10)
-    convolve(0, 32)
-    finish(1)
-    lift(27, 5)
-    convolve(81, 16)
-    finish(2)
+            outgoing[:, half * 3 + i] = sent.reshape(lat_count, 3, MOST, LANES)
+
+    def send(t, carry):
+        target = (me + t) % lat_count
+        pltpu.make_async_remote_copy(
+            src_ref=outgoing.at[target],
+            dst_ref=incoming.at[me],
+            send_sem=out_send,
+            recv_sem=out_recv,
+            device_id={"lat": target, "lon": lon},
+            device_id_type=MESH,
+        ).start()
+        return carry
+
+    lax.fori_loop(1, lat_count, send, 0)
+    incoming[me] = outgoing[me]
 
     rest = pl.ds(0, lat_count - 1)
-    for n, (tile, tiles) in enumerate(PARTS):
-        block = incoming.at[pl.ds(tile, tiles), rest]
-        pltpu.make_async_copy(block, block, out_recv.at[n]).wait()
-        for i in range(tiles):
-            landed = incoming[tile + i].reshape(lat_count * SENT, LANES)
-            made = dot(gather[...], landed)
-            for a in range(3):
-                at = pl.ds((tile + i) * LANES, LANES)
-                out_ref[a, :, at] = made[a * slots : (a + 1) * slots].astype(BF)
+    pltpu.make_async_copy(incoming.at[rest], incoming.at[rest], out_recv).wait()
+    for i in range(6):
+        landed = incoming[:, i].reshape(lat_count * SENT, LANES)
+        made = dot(gather[...], landed).astype(BF)
+        for a in range(3):
+            out_ref[a, :, i * LANES : (i + 1) * LANES] = made[a * slots : (a + 1) * slots]
     for copy in copies:
         copy.wait_send()
-    for n, (tile, tiles) in enumerate(PARTS):
-        block = outgoing.at[pl.ds(tile, tiles), rest]
-        pltpu.make_async_copy(block, block, out_send.at[n]).wait()
+    pltpu.make_async_copy(outgoing.at[rest], outgoing.at[rest], out_send).wait()
 
 
 def body(lat_count, lon_count, coarse, ocean_mask, band_plan, up_weight, up_bias, first_weight,
          first_bias, second_weight, second_bias, head_weight, head_bias):
     slots = 32
+    width = coarse.shape[1]
     vmem = pl.BlockSpec(memory_space=pltpu.VMEM)
     row = lambda v: v.reshape(1, -1)
     made = pl.pallas_call(
@@ -430,8 +415,8 @@
         in_specs=[vmem] * 11,
         out_specs=vmem,
         scratch_shapes=[
-            pltpu.VMEM((2, 1, coarse.shape[1]), F32),
-            pltpu.VMEM((2, 1, coarse.shape[1]), F32),
+            pltpu.VMEM((2, 1, width), F32),
+            pltpu.VMEM((2, 1, width), F32),
             pltpu.VMEM((2, 2, 1, LANES), F32),
             pltpu.VMEM((2, ROWS, LANES), BF),
             pltpu.VMEM((PAIRS, ROWS, LANES), BF),
@@ -445,12 +430,12 @@
             pltpu.VMEM((2, ROWS, LANES), BF),
             pltpu.VMEM((lat_count * SENT, 3 * ROWS), BF),
             pltpu.VMEM((3 * slots, lat_count * SENT), BF),
-            pltpu.VMEM((6, lat_count, 3, MOST, LANES), BF),
-            pltpu.VMEM((6, lat_count, 3, MOST, LANES), BF),
+            pltpu.VMEM((lat_count, 6, 3, MOST, LANES), BF),
+            pltpu.VMEM((lat_count, 6, 3, MOST, LANES), BF),
             pltpu.SemaphoreType.DMA((8,)),
             pltpu.SemaphoreType.DMA((8,)),
-            pltpu.SemaphoreType.DMA((len(PARTS),)),
-            pltpu.SemaphoreType.DMA((len(PARTS),)),
+            pltpu.SemaphoreType.DMA,
+            pltpu.SemaphoreType.DMA,
         ],
         compiler_params=pltpu.CompilerParams(
             collective_id=0, has_side_effects=True, vmem_limit_bytes=60 * 2**20

time: 55.1 us -> 56.2 us (1.020)
  the two profiles are of different devices: /device:TPU:2 before, /device:TPU:64 now
where the time goes in v5:
time: 56.2 us; the launch traced here: 56.1 us
  Pallas kernels  54.4 us (97%)
  other arithmetic  1.64 us (3%)
    pallas_call x1, Pallas kernels, body(): pl.pallas_call(partial(kernel, lat_count, lon_count), out_shape=jax.Shape...  54.4 us
    convert_element_type x1, other arithmetic, body(): return made.transpose(1, 0, 2).astype(F32)  1.64 us

profile of v5, /device:TPU:64, one launch (start us, length us, event | category | flops | bytes accessed | tf_op | source)
XLA Modules:
  0.0 56.1 jit_solution(6988894435928112594)
XLA Ops:
  0.0 54.4 %shard_map.109 = bf16[3,32,768]{2,1,0:T(8,128)(2,1)} custom-call(bf16[64,4096]{1,0:T(8,128)(2,1)} %x_ref.1, s32[16,128]{1,0:T(8,128)} %bitcast.9, s32[16,128]{1,0:T(8,128)} %bitcast.10, bf16[3,3,64,64]{3,2,1,0:T(8,128)(2,1)} %up_weight.1, f32[1,64]{1,0:T(1,128)} %bitcast.12, bf16[3,3,64,64]{3,2,1,0:T(8,128)(2,1)} %first_weight.1, f32[1,64]{1,0:T(1,128)} %bitcast.13, ...), custom_call_target="tpu_custom_call" | custom-call | tf_op jit(solution)/shard_map/pallas_call | solution.py:412
  54.4 1.6 %convert_bitcast_fusion = f32[32,3,768]{2,0,1:T(8,128)} fusion(bf16[3,32,768]{2,1,0:T(8,128)(2,1)} %shard_map.109), kind=kLoop, calls=%fused_computation | loop fusion | flops 73728 | bytes 442368 | tf_op jit(solution)/shard_map/convert_element_type | solution.py:456
